TPU v7x, 128 devices: a whole 4x4x4 slice. The times are simulated.
128 devices in a mesh: rows: 32 (over x, y, z_hi), cols: 4 (over z_lo, core).
Axes of the slice: x: 4, y: 4, z: 4 (z_hi: 2, z_lo: 2; z = z_hi * 2 + z_lo), core: 2. Of those that a mesh axis runs over, the one named last changes fastest.
Arguments:
- queries: bfloat16 [256, 1536, 128], P('rows', 'cols'), may hold values from -3 to 3
- keys: bfloat16 [256, 1536, 128], P('rows', 'cols'), may hold values from -3 to 3
- values: bfloat16 [256, 1536, 128], P('rows', 'cols'), may hold values from -4 to 4
- out_grad: bfloat16 [256, 1536, 128], P('rows', 'cols'), may hold values from -16 to 16
- pair_bias: bfloat16 [1536, 4, 1536], P(None, None, 'cols'), may hold values from -4 to 4
- token_mask: int32 [1536], replicated, may hold values from 0 to 1, as said below
- span_index: int32 [32], P('rows'), may hold values from 0 to 191
Outputs:
- query_grad: bfloat16 [256, 1536, 128], P('rows', 'cols')
- key_grad: bfloat16 [256, 1536, 128], P('rows', 'cols')
- value_grad: bfloat16 [256, 1536, 128], P('rows', 'cols')
- bias_grad: float32 [1536, 4, 1536], P('rows', None, 'cols')
Inputs may be any that keep to these rules, and one draw needn't show every extreme that they name: `token_mask`: every aligned block of 8 tokens holds a 1.
All inputs are finite; a program needn't handle non-finite values.
Results may differ from a plain program's by a relative error of at most 0.005.
Values may be sent and summed in bfloat16 or wider, within the bound.
No kernel may reach another device: no remote copies, remote signals or barrier semaphores. Data moves between devices by JAX's collectives and lax.ppermute only.
A program may use at most 192 MiB of HBM per device.

v0:
```python
import functools

import jax
import jax.numpy as jnp
from jax import lax
from jax.experimental import pallas as pl
from jax.experimental.pallas import tpu as pltpu
from jax.sharding import PartitionSpec as P

HEADS = 4
HEAD_DIM = 32
CH = HEADS * HEAD_DIM
SCALE = HEAD_DIM**-0.5
LOG2E = 1.4426950408889634
CHUNKS = 3
TILE = 256
VMEM = 60 * 2**20
NT = (((1,), (1,)), ((), ()))
F32 = jnp.float32
BF16 = jnp.bfloat16


def only_head(x, h):
    lane = lax.broadcasted_iota(jnp.int32, x.shape, 1)
    return jnp.where((lane // HEAD_DIM) == h, x, jnp.zeros_like(x))


def joined(parts, which):
    return jnp.concatenate([part[which, 0] for part in parts], axis=0)


def bias_block(parts):
    parts = [part[0, :, 0].reshape(-1, part.shape[-1]) for part in parts]
    return jnp.concatenate(parts, axis=0).astype(F32) * LOG2E


def totals_kernel(col_ref, *refs):
    n = (len(refs) - 6) // 2
    parts, biases, (k_ref, v_ref, gate_ref, out_ref, e_ref, bias_ref) = refs[:n], refs[n : 2 * n], refs[2 * n :]
    q, g = joined(parts, 0), joined(parts, 1)
    k = k_ref[0]
    key_len = k.shape[0]

    @pl.when(pl.program_id(0) == 0)
    def start():
        bias = bias_block(biases)
        gate = jnp.concatenate([gate_ref[...]] * (q.shape[0] // CH), axis=1)
        for h in range(HEADS):
            bias_ref[h] = bias[:, h * key_len : (h + 1) * key_len].T + gate

    for h in range(HEADS):
        s = lax.dot_general(k, only_head(q, h), NT, preferred_element_type=F32)
        e_ref[h] = jnp.exp2(s * (SCALE * LOG2E) + bias_ref[h]).astype(BF16)
    gt = g.T.astype(F32)
    vt = v_ref[0].T
    ones = jnp.ones((16, key_len), BF16)
    for h in range(HEADS):
        rows = slice(h * HEAD_DIM, (h + 1) * HEAD_DIM)
        o = jnp.dot(jnp.concatenate([vt[rows], ones], axis=0), e_ref[h], preferred_element_type=F32)
        total = o[HEAD_DIM : HEAD_DIM + 1]
        weighted = jnp.sum(o[:HEAD_DIM] * gt[rows], axis=0, keepdims=True)
        for u in range(n):
            at = slice(u * (q.shape[0] // n), (u + 1) * (q.shape[0] // n))
            out_ref[col_ref[0] ^ u, 0, h : h + 1] = total[:, at]
            out_ref[col_ref[0] ^ u, 0, HEADS + h : HEADS + h + 1] = weighted[:, at]


def part_specs(part_len, bias, chunk):
    _, owners, _, step, width = bias.shape
    data = [pl.BlockSpec((2, 1, part_len, CH), lambda i, col: (0, i, 0, 0))] * 4
    return data + [
        pl.BlockSpec((1, owners, 1, step, width), lambda i, col, u=u: (col[0] ^ u, 0, chunk, 0, 0)) for u in range(4)
    ]


def totals(col, parts, bias, chunk, keys, values, key_gate):
    rows, key_len, _ = keys.shape
    part_len = parts[0].shape[2]
    n = len(parts)
    count = n * part_len
    per_row = lambda i, col: (i, 0, 0)
    work = rows * count * HEADS * key_len
    return pl.pallas_call(
        totals_kernel,
        grid_spec=pltpu.PrefetchScalarGridSpec(
            num_scalar_prefetch=1,
            grid=(rows,),
            in_specs=part_specs(part_len, bias, chunk)
            + [
                pl.BlockSpec((1, key_len, CH), per_row),
                pl.BlockSpec((1, key_len, CH), per_row),
                pl.BlockSpec((key_len, CH), lambda i, col: (0, 0)),
            ],
            out_specs=pl.BlockSpec((n, 1, 2 * HEADS, part_len), lambda i, col: (0, i, 0, 0)),
            scratch_shapes=[pltpu.VMEM((HEADS, key_len, count), BF16), pltpu.VMEM((HEADS, key_len, count), F32)],
        ),
        out_shape=jax.ShapeDtypeStruct((n, rows, 2 * HEADS, part_len), F32),
        compiler_params=pltpu.CompilerParams(vmem_limit_bytes=VMEM),
        cost_estimate=pl.CostEstimate(flops=work * 512 * 3, bytes_accessed=2**20, transcendentals=work),
        name="totals",
    )(col, *parts, *[bias] * n, keys, values, key_gate)


def split(x):
    a = x.astype(BF16)
    rest = x - a.astype(F32)
    b = rest.astype(BF16)
    return [y.astype(F32) for y in (a, b, (rest - b.astype(F32)).astype(BF16))]


def grads_kernel(first, last, col_ref, *refs):
    parts, biases, refs = refs[:4], refs[4:8], refs[8:]
    k_ref, v_ref, gate_ref, *refs = refs
    stats, refs = refs[:4], refs[4:]
    col = col_ref[0]
    if not first:
        dk_in, dv_in, *refs = refs
    dq_refs, refs = refs[:2], refs[2:]
    dk_out, dv_out, db_ref, kx_ref, vx_ref, sum_ref, p_ref, ds_ref, dk_ref, dv_ref, bias_ref = refs
    i = pl.program_id(0)
    q, g = joined(parts, 0), joined(parts, 1)
    count, key_len = q.shape[0], k_ref.shape[1]
    width = HEADS * key_len

    @pl.when(i == 0)
    def start():
        sum_ref[...] = jnp.zeros(sum_ref.shape, F32)
        bias_ref[...] = bias_block(biases) + jnp.concatenate([gate_ref[:1]] * HEADS, axis=1)
        lane = lax.broadcasted_iota(jnp.int32, (key_len, CH), 1)
        for h in range(HEADS):
            rows = slice(h * key_len, (h + 1) * key_len)
            for ref, at in ((kx_ref, h), (vx_ref, HEADS + h)):
                hit = (lane < 6 * HEADS) & (lane % (2 * HEADS) == at)
                ref[rows, CH:] = jnp.where(hit, -1.0, 0.0).astype(BF16)

    k, v = k_ref[0], v_ref[0]
    for h in range(HEADS):
        rows = slice(h * key_len, (h + 1) * key_len)
        kx_ref[rows, :CH] = only_head(k, h)
        vx_ref[rows, :CH] = only_head(v, h)

    stat = [sum(ref[col ^ u, 0] for ref in stats[1:]) + stats[0][col ^ u, 0] for u in range(4)]
    stat = jnp.concatenate(stat, axis=1)
    total = stat[:HEADS]
    level = jnp.log(total) * (1.0 / SCALE)
    delta = stat[HEADS:] / total
    pieces = split(jnp.concatenate([level, delta], axis=0))
    extra = jnp.concatenate(pieces + [jnp.zeros((CH - 6 * HEADS, count), F32)], axis=0).T.astype(BF16)
    qx = jnp.concatenate([q, extra], axis=1)
    gx = jnp.concatenate([g, extra], axis=1)
    qt, gt = q.T, g.T
    dq = jnp.zeros((count, CH), F32)
    for n in range(width // TILE):
        at = slice(n * TILE, (n + 1) * TILE)
        s = lax.dot_general(qx, kx_ref[at], NT, preferred_element_type=F32)
        t = lax.dot_general(gx, vx_ref[at], NT, preferred_element_type=F32)
        p = jnp.exp2(s * (SCALE * LOG2E) + bias_ref[:, at])
        ds = p * t
        sum_ref[:, at] += ds
        low = ds.astype(BF16)
        p_ref[:, at] = p.astype(BF16)
        ds_ref[:, at] = low
        dq = dq + jnp.dot(low, kx_ref[at, :CH], preferred_element_type=F32)
    dq = (dq * SCALE).astype(BF16)
    part_len = count // 4
    for u in range(4):
        dq_refs[u % 2][u // 2, 0] = dq[u * part_len : (u + 1) * part_len]
    for h in range(HEADS):
        rows, at = slice(h * HEAD_DIM, (h + 1) * HEAD_DIM), slice(h * key_len, (h + 1) * key_len)
        dv = jnp.dot(gt[rows], p_ref[:, at], preferred_element_type=F32)
        dk = jnp.dot(qt[rows], ds_ref[:, at], preferred_element_type=F32)
        if not first:
            dv, dk = dv + dv_in[0, rows], dk + dk_in[0, rows]
        if last:
            dv_ref[rows] = dv
            dk_ref[rows] = dk * SCALE
        else:
            dv_out[0, rows] = dv
            dk_out[0, rows] = dk
    if last:
        dv_out[0] = dv_ref[...].T.astype(BF16)
        dk_out[0] = dk_ref[...].T.astype(BF16)

    @pl.when(i == pl.num_programs(0) - 1)
    def finish():
        for u in range(4):
            part = sum_ref[u * part_len : (u + 1) * part_len].astype(BF16)
            db_ref[col ^ u] = part.reshape(db_ref.shape[1:])


def grads(col, parts, bias, chunk, keys, values, row_gate, stats, carried, last):
    rows, key_len, _ = keys.shape
    part_len = parts[0].shape[2]
    count, width = 4 * part_len, HEADS * key_len
    per_row = lambda i, col: (i, 0, 0)
    whole = lambda i, col: (0, 0)
    share = (bias.shape[1], bias.shape[3], width)
    side = pl.BlockSpec((1, CH, key_len), per_row)
    side_shape = jax.ShapeDtypeStruct((rows, CH, key_len), F32)
    final = pl.BlockSpec((1, key_len, CH), per_row)
    final_shape = jax.ShapeDtypeStruct((rows, key_len, CH), BF16)
    work = rows * count * width
    return pl.pallas_call(
        functools.partial(grads_kernel, not carried, last),
        grid_spec=pltpu.PrefetchScalarGridSpec(
            num_scalar_prefetch=1,
            grid=(rows,),
            in_specs=part_specs(part_len, bias, chunk)
            + [
                pl.BlockSpec((1, key_len, CH), per_row),
                pl.BlockSpec((1, key_len, CH), per_row),
                pl.BlockSpec((8, key_len), whole),
            ]
            + [pl.BlockSpec((4, 1, 2 * HEADS, part_len), lambda i, col: (0, i, 0, 0))] * 4
            + [side] * len(carried),
            out_specs=[
                *[pl.BlockSpec((2, 1, part_len, CH), lambda i, col: (0, i, 0, 0))] * 2,
                final if last else side,
                final if last else side,
                pl.BlockSpec((4,) + share, lambda i, col: (0, 0, 0, 0)),
            ],
            scratch_shapes=[
                pltpu.VMEM((width, 2 * CH), BF16),
                pltpu.VMEM((width, 2 * CH), BF16),
                pltpu.VMEM((count, width), F32),
                pltpu.VMEM((count, width), BF16),
                pltpu.VMEM((count, width), BF16),
                pltpu.VMEM((CH, key_len), F32),
                pltpu.VMEM((CH, key_len), F32),
                pltpu.VMEM((count, width), F32),
            ],
        ),
        out_shape=[
            *[jax.ShapeDtypeStruct((2, rows, part_len, CH), BF16)] * 2,
            final_shape if last else side_shape,
            final_shape if last else side_shape,
            jax.ShapeDtypeStruct((4,) + share, BF16),
        ],
        compiler_params=pltpu.CompilerParams(vmem_limit_bytes=VMEM),
        cost_estimate=pl.CostEstimate(flops=work * 512 * 6, bytes_accessed=2**20, transcendentals=work),
        name="grads",
    )(col, *parts, *[bias] * 4, keys, values, row_gate, *stats, *carried)


def partner(x, distance):
    return lax.ppermute(x, "cols", [(c, c ^ distance) for c in range(4)])


def per_device(queries, keys, values, out_grad, pair_bias, token_mask, span_index):
    rows, key_len, _ = keys.shape
    col = lax.axis_index("cols")
    owners = 8
    span = key_len // owners
    step = span // CHUNKS
    part_len = owners * step
    count = 4 * part_len
    width = HEADS * key_len

    row_keep = lax.dynamic_slice_in_dim(token_mask, span_index[0] * rows, rows)
    masked = out_grad * row_keep.astype(BF16)[:, None, None]
    pairs = jnp.stack([queries, masked]).reshape(2, rows, owners, CHUNKS, step, CH)

    key_keep = lax.dynamic_slice_in_dim(token_mask, col * key_len, key_len) > 0
    gate = jnp.where(key_keep, F32(0.0), F32(-1e30))
    key_gate = jnp.broadcast_to(gate[:, None], (key_len, CH))
    row_gate = jnp.broadcast_to(gate[None, :], (8, key_len))
    bias = jnp.concatenate([pair_bias[:, h] for h in range(HEADS)], axis=1).reshape(4, owners, CHUNKS, step, width)
    col_id = col.astype(jnp.int32).reshape(1)

    tie = lax.optimization_barrier
    owns = [pairs[:, :, :, b].reshape(2, rows, part_len, CH) for b in range(CHUNKS)]

    def spread(own, far):
        return [own, partner(own, 1), far, partner(far, 1)]

    def call_totals(b):
        return totals(col_id, parts[b], bias, b, keys, values, key_gate)

    def all_stats(stat):
        return [stat] + [partner(stat, distance) for distance in (1, 2, 3)]

    def call_grads(b, stats, carried):
        *dq, dk, dv, db = grads(
            col_id, parts[b], bias, b, keys, values, row_gate, stats, carried, b == CHUNKS - 1
        )
        return dq, (dk, dv), db.reshape(32, step, width)

    def near_queries(dq):
        pair = dq[0].astype(F32) + partner(dq[1], 1).astype(F32)
        return pair[0], pair[1].astype(BF16)

    def far_queries(pair):
        return (pair[0] + partner(pair[1], 2).astype(F32)).astype(BF16)

    def swap_bias(db):
        return lax.all_to_all(db, "rows", 0, 0, tiled=True)

    def summed(terms):
        return jnp.sum(terms.astype(F32), axis=0)

    far0, bias = tie((partner(owns[0], 2), bias))
    far0, owns[1] = tie((far0, owns[1]))
    far1 = partner(owns[1], 2)
    parts = [spread(owns[0], far0), None, None]
    t0 = call_totals(0)
    far1, owns[2], t0 = tie((far1, owns[2], t0))
    far2 = partner(owns[2], 2)
    parts[1] = spread(owns[1], far1)
    t1 = call_totals(1)
    far2, t1, s0 = tie((far2, t1, all_stats(t0)))
    parts[2] = spread(owns[2], far2)
    t2 = call_totals(2)
    t2, s0, s1 = tie((t2, s0, all_stats(t1)))
    dq0, carried, db0 = call_grads(0, s0, ())
    dq0, db0, s1, s2 = tie((dq0, db0, s1, all_stats(t2)))
    dq1, carried, db1 = call_grads(1, s1, carried)
    n0, db0, dq1, db1 = tie((near_queries(dq0), swap_bias(db0), dq1, db1))
    dq2, carried, db2 = call_grads(2, s2, carried)
    q0, n1, db1, dq2, db2 = tie((far_queries(n0), near_queries(dq1), swap_bias(db1), dq2, db2))
    n2, db2 = tie((near_queries(dq2), db2))
    db2 = swap_bias(db2)
    q1, q2 = far_queries(n1), far_queries(n2)
    b0, b1, b2 = [summed(db) for db in (db0, db1, db2)]
    key_grad, value_grad = carried
    query_grad = jnp.stack([q0, q1, q2]).reshape(CHUNKS, rows, owners, step, CH)
    query_grad = query_grad.transpose(1, 2, 0, 3, 4).reshape(rows, key_len, CH)
    bias_grad = jnp.concatenate([b0, b1, b2], axis=0).reshape(span, HEADS, key_len)
    return (query_grad, key_grad, value_grad, bias_grad)


def solution(mesh):
    return jax.shard_map(
        per_device,
        mesh=mesh,
        in_specs=(
            P("rows", "cols", None),
            P("rows", "cols", None),
            P("rows", "cols", None),
            P("rows", "cols", None),
            P(None, None, "cols"),
            P(),
            P("rows"),
        ),
        out_specs=(
            P("rows", "cols", None),
            P("rows", "cols", None),
            P("rows", "cols", None),
            P("rows", None, "cols"),
        ),
        check_vma=False,
    )
```

profile of v0, /device:TPU:1, one launch (start us, length us, event | category | flops | bytes accessed | tf_op | source)
XLA Modules:
  0.0 211.5 jit_solution(4253695896639263659)
XLA Ops:
  1.3 0.8 dynamic-slice_convert_fusion
  2.0 1.4 broadcast_multiply_fusion
  3.5 1.5 pad_maximum_fusion.1
  5.0 1.5 collective-permute-start
  6.5 1.7 collective-permute-start.1
  8.2 6.8 %fusion.6 = (bf16[1536,1,384]{2,1,0:T(2,128)(2,1)S(1)}, bf16[1536,1,384]{2,1,0:T(2,128)(2,1)S(1)}, bf16[1536,1,384]{2,1,0:T(2,128)(2,1)S(1)}, bf16[1536,1,384]{2,1,0:T(2,128)(2,1)S(1)}) fusion(bf16[1536,4,384]{2,1,0:T(4,128)(2,1)S(1)} %copy-done), kind=kLoop, calls=%fused_computation.32 | loop fusion | bytes 9437184 | tf_op jit(solution)/shard_map/slice | solution.py:267
  15.9 2.5 %pad_maximum_fusion.refs_4_.refs_5_.refs_6_.refs_7_ = bf16[4,8,3,16,1536]{4,3,2,1,0:T(8,128)(2,1)} fusion(bf16[4,8,3,16,384]{4,3,2,1,0:T(8,128)(2,1)S(1)} %bitcast.38, bf16[4,8,3,16,384]{4,3,2,1,0:T(8,128)(2,1)S(1)} %bitcast.39, bf16[4,8,3,16,384]{4,3,2,1,0:T(8,128)(2,1)S(1)} %bitcast.40, bf16[4,8,3,16,384]{4,3,2,1,0:T(8,128)(2,1)S(1)} %bitcast.41), kind=kLoop, calls=%fused_computation | loop fusion | flops 18874368 | bytes 9437184 | tf_op jit(solution)/shard_map/concatenate | solution.py:267
  18.5 2.0 collective-permute-done.1.refs_2_
  20.4 0.7 collective-permute-start.2
  21.1 0.8 fusion.5
  21.9 1.5 collective-permute-start.3
  23.7 0.8 broadcast_in_dim.24.refs_10_
  24.5 11.1 %totals.3.refs_11_ = f32[4,8,8,128]{3,2,1,0:T(8,128)} custom-call(s32[1]{0:T(128)} %bitcast.col_ref, bf16[2,8,128,128]{3,2,1,0:T(8,128)(2,1)} %bitcast.61, bf16[2,8,128,128]{3,2,1,0:T(8,128)(2,1)} %copy-done.10, bf16[2,8,128,128]{3,2,1,0:T(8,128)(2,1)} %copy-done.11, bf16[2,8,128,128]{3,2,1,0:T(8,128)(2,1)} %collective-permute-done.2.refs_3_, ...), custom_call_target="tpu_custom_call" | custom-call | flops 9663676416 | bytes 1048576 | tf_op jit(solution)/shard_map/totals/pallas_call | solution.py:83
  36.3 1.4 collective-permute-start.5
  37.7 0.8 collective-permute-start.8
  38.5 1.6 collective-permute-start.10
  40.1 11.2 %totals.4.refs_11_ = f32[4,8,8,128]{3,2,1,0:T(8,128)} custom-call(s32[1]{0:T(128)} %bitcast.col_ref, bf16[2,8,128,128]{3,2,1,0:T(8,128)(2,1)} %bitcast.57, bf16[2,8,128,128]{3,2,1,0:T(8,128)(2,1)} %collective-permute-done.6.refs_1_, bf16[2,8,128,128]{3,2,1,0:T(8,128)(2,1)} %copy-done.12, bf16[2,8,128,128]{3,2,1,0:T(8,128)(2,1)} %copy-done.14, ...), custom_call_target="tpu_custom_call" | custom-call | flops 9663676416 | bytes 1048576 | tf_op jit(solution)/shard_map/totals/pallas_call | solution.py:83
  51.3 0.8 collective-permute-done.9.refs_13_
  52.1 3.4 %collective-permute-done.10.refs_14_ = f32[4,8,8,128]{3,2,1,0:T(8,128)S(1)} collective-permute-done((f32[4,8,8,128]{3,2,1,0:T(8,128)}, f32[4,8,8,128]{3,2,1,0:T(8,128)S(1)}, u32[]{:S(2)}, u32[]{:S(2)}) %collective-permute-start.10) | collective-permute-done | bytes 131104 | tf_op jit(solution)/shard_map/ppermute | solution.py:246
  56.1 1.4 collective-permute-start.13
  57.9 0.8 copy-done.8
  58.7 0.8 copy-done.13
  59.5 11.1 %totals.5.refs_11_ = f32[4,8,8,128]{3,2,1,0:T(8,128)} custom-call(s32[1]{0:T(128)} %bitcast.col_ref, bf16[2,8,128,128]{3,2,1,0:T(8,128)(2,1)} %bitcast.53, bf16[2,8,128,128]{3,2,1,0:T(8,128)(2,1)} %copy-done.8, bf16[2,8,128,128]{3,2,1,0:T(8,128)(2,1)} %copy-done.9, bf16[2,8,128,128]{3,2,1,0:T(8,128)(2,1)} %copy-done.13, ...), custom_call_target="tpu_custom_call" | custom-call | flops 9663676416 | bytes 1048576 | tf_op jit(solution)/shard_map/totals/pallas_call | solution.py:83
  71.1 1.4 collective-permute-start.16
  73.7 20.1 %grads.3 = (bf16[2,8,128,128]{3,2,1,0:T(8,128)(2,1)}, bf16[2,8,128,128]{3,2,1,0:T(8,128)(2,1)}, f32[8,128,384]{2,1,0:T(8,128)}, f32[8,128,384]{2,1,0:T(8,128)}, bf16[4,8,16,1536]{3,2,1,0:T(8,128)(2,1)}) custom-call(s32[1]{0:T(128)} %bitcast.col_ref, bf16[2,8,128,128]{3,2,1,0:T(8,128)(2,1)} %bitcast.62, bf16[2,8,128,128]{3,2,1,0:T(8,128)(2,1)} %copy-done.10, ...), custom_call_target="tpu_custom_call" | custom-call | flops 19327352832 | bytes 1048576 | tf_op jit(solution)/shard_map/grads/pallas_call | solution.py:203
  94.6 10.1 %all-to-all-start = ((bf16[32,16,1536]{2,1,0:T(8,128)(2,1)}), bf16[32,16,1536]{2,1,0:T(8,128)(2,1)S(1)}, u32[]{:S(2)}, u32[]{:S(2)}) async-start(bf16[32,16,1536]{2,1,0:T(8,128)(2,1)} %bitcast.45), calls=%async_computation | async-start | bytes 3145728 | tf_op jit(solution)/shard_map/all_to_all | solution.py:296
  104.7 20.4 %grads.4 = (bf16[2,8,128,128]{3,2,1,0:T(8,128)(2,1)}, bf16[2,8,128,128]{3,2,1,0:T(8,128)(2,1)}, f32[8,128,384]{2,1,0:T(8,128)}, f32[8,128,384]{2,1,0:T(8,128)}, bf16[4,8,16,1536]{3,2,1,0:T(8,128)(2,1)}) custom-call(s32[1]{0:T(128)} %bitcast.col_ref, bf16[2,8,128,128]{3,2,1,0:T(8,128)(2,1)} %bitcast.58, ...), custom_call_target="tpu_custom_call" | custom-call | flops 19327352832 | bytes 1048576 | tf_op jit(solution)/shard_map/grads/pallas_call | solution.py:203
  125.3 0.8 slice_bitcast_fusion.2
  126.2 2.2 %all-to-all-done = bf16[32,16,1536]{2,1,0:T(8,128)(2,1)S(1)} async-done(((bf16[32,16,1536]{2,1,0:T(8,128)(2,1)}), bf16[32,16,1536]{2,1,0:T(8,128)(2,1)S(1)}, u32[]{:S(2)}, u32[]{:S(2)}) %all-to-all-start) | async-done | bytes 1572896 | tf_op jit(solution)/shard_map/all_to_all | solution.py:296
  128.4 0.7 collective-permute-start.19
  129.2 2.0 collective-permute-start.20
  131.1 7.0 %all-to-all-start.1 = ((bf16[32,16,1536]{2,1,0:T(8,128)(2,1)}), bf16[32,16,1536]{2,1,0:T(8,128)(2,1)S(1)}, u32[]{:S(2)}, u32[]{:S(2)}) async-start(bf16[32,16,1536]{2,1,0:T(8,128)(2,1)} %bitcast.44), calls=%async_computation.1 | async-start | bytes 3145728 | tf_op jit(solution)/shard_map/all_to_all | solution.py:296
  138.1 21.4 %grads.5 = (bf16[2,8,128,128]{3,2,1,0:T(8,128)(2,1)}, bf16[2,8,128,128]{3,2,1,0:T(8,128)(2,1)}, bf16[8,384,128]{2,1,0:T(8,128)(2,1)}, bf16[8,384,128]{2,1,0:T(8,128)(2,1)}, bf16[4,8,16,1536]{3,2,1,0:T(8,128)(2,1)}) custom-call(s32[1]{0:T(128)} %bitcast.col_ref, bf16[2,8,128,128]{3,2,1,0:T(8,128)(2,1)} %bitcast.54, bf16[2,8,128,128]{3,2,1,0:T(8,128)(2,1)} %copy-done.8, ...), custom_call_target="tpu_custom_call" | custom-call | flops 19327352832 | bytes 1048576 | tf_op jit(solution)/shard_map/grads/pallas_call | solution.py:203
  159.6 1.0 add_convert_fusion.2
  160.6 1.3 convert_add_fusion.1
  161.9 0.8 fusion.3
  162.7 0.8 slice_bitcast_fusion.1
  163.8 1.9 collective-permute-done.22
  165.7 1.2 convert_add_fusion
  166.8 0.8 slice_bitcast_fusion
  167.7 0.7 fusion.4
  168.4 9.5 %all-to-all-start.2 = ((bf16[32,16,1536]{2,1,0:T(8,128)(2,1)}), bf16[32,16,1536]{2,1,0:T(8,128)(2,1)}, u32[]{:S(2)}, u32[]{:S(2)}) async-start(bf16[32,16,1536]{2,1,0:T(8,128)(2,1)} %bitcast.43), calls=%async_computation.2 | async-start | bytes 3145728 | tf_op jit(solution)/shard_map/all_to_all | solution.py:296
  178.3 1.5 collective-permute-start.23
  180.0 22.3 %collective-permute-done.21 = bf16[8,128,128]{2,1,0:T(8,128)(2,1)S(1)} collective-permute-done((bf16[8,128,128]{2,1,0:T(8,128)(2,1)}, bf16[8,128,128]{2,1,0:T(8,128)(2,1)S(1)}, u32[]{:S(2)}, u32[]{:S(2)}) %collective-permute-start.21) | collective-permute-done | bytes 262176 | tf_op jit(solution)/shard_map/ppermute | solution.py:246
  202.4 5.4 %collective-permute-done.23 = bf16[8,128,128]{2,1,0:T(8,128)(2,1)S(1)} collective-permute-done((bf16[8,128,128]{2,1,0:T(8,128)(2,1)}, bf16[8,128,128]{2,1,0:T(8,128)(2,1)S(1)}, u32[]{:S(2)}, u32[]{:S(2)}) %collective-permute-start.23) | collective-permute-done | bytes 262176 | tf_op jit(solution)/shard_map/ppermute | solution.py:246
  208.0 1.0 copy.20
  209.0 1.6 convert_reduce_fusion
  210.7 0.8 reshape.60
  (91 shorter events, 6.2 us)
Async XLA Ops:
  2.0 6.2 %copy-start = (bf16[1536,4,384]{2,1,0:T(4,128)(2,1)S(1)}, bf16[1536,4,384]{2,1,0:T(4,128)(2,1)}, u32[]{:S(2)}) copy-start(bf16[1536,4,384]{2,1,0:T(4,128)(2,1)} %param.11) | copy-start | bytes 14155780
  5.0 10.1 %copy-start.6 = (bf16[2,8,8,1,16,128]{5,4,3,2,1,0:T(8,128)(2,1)}, bf16[2,8,8,1,16,128]{5,4,3,2,1,0:T(8,128)(2,1)S(1)}, u32[]{:S(2)}) copy-start(bf16[2,8,8,1,16,128]{5,4,3,2,1,0:T(8,128)(2,1)S(1)} %get-tuple-element.137) | copy-start | bytes 1572868
  5.0 18.4 %copy-start.5 = (bf16[2,8,8,1,16,128]{5,4,3,2,1,0:T(8,128)(2,1)}, bf16[2,8,8,1,16,128]{5,4,3,2,1,0:T(8,128)(2,1)S(1)}, u32[]{:S(2)}) copy-start(bf16[2,8,8,1,16,128]{5,4,3,2,1,0:T(8,128)(2,1)S(1)} %get-tuple-element.138) | copy-start | bytes 1572868
  5.0 31.3 %copy-start.4 = (bf16[2,8,8,1,16,128]{5,4,3,2,1,0:T(8,128)(2,1)}, bf16[2,8,8,1,16,128]{5,4,3,2,1,0:T(8,128)(2,1)S(1)}, u32[]{:S(2)}) copy-start(bf16[2,8,8,1,16,128]{5,4,3,2,1,0:T(8,128)(2,1)S(1)} %get-tuple-element.136) | copy-start | bytes 1572868
  5.0 18.7 %collective-permute-start = (bf16[2,8,128,128]{3,2,1,0:T(8,128)(2,1)S(1)}, bf16[2,8,128,128]{3,2,1,0:T(8,128)(2,1)S(1)}, u32[]{:S(2)}, u32[]{:S(2)}) collective-permute-start(bf16[2,8,128,128]{3,2,1,0:T(8,128)(2,1)S(1)} %bitcast.59), channel_id=1, source_target_pairs={{0,1},{1,0},{2,3},{3,2},{4,5},{5,4},{6,7},{7,6},{8,9},{9,8},{10,11... | collective-permute-start | bytes 1572872 | tf_op jit(solution)/shard_map/ppermute | solution.py:246
  6.5 13.9 %collective-permute-start.1 = (bf16[2,8,128,128]{3,2,1,0:T(8,128)(2,1)S(1)}, bf16[2,8,128,128]{3,2,1,0:T(8,128)(2,1)S(1)}, u32[]{:S(2)}, u32[]{:S(2)}) collective-permute-start(bf16[2,8,128,128]{3,2,1,0:T(8,128)(2,1)S(1)} %bitcast.60), channel_id=1, source_target_pairs={{0,2},{1,3},{2,0},{3,1},{4,6},{5,7},{6,4},{7,5},{8,10},{9,11},{10,... | collective-permute-start | bytes 1572872 | tf_op jit(solution)/shard_map/ppermute | solution.py:246
  20.4 4.1 %copy-start.11 = (bf16[2,8,128,128]{3,2,1,0:T(8,128)(2,1)}, bf16[2,8,128,128]{3,2,1,0:T(8,128)(2,1)S(1)}, u32[]{:S(2)}) copy-start(bf16[2,8,128,128]{3,2,1,0:T(8,128)(2,1)S(1)} %collective-permute-done.1.refs_2_) | copy-start | bytes 1572868
  20.4 3.3 %collective-permute-start.2 = (bf16[2,8,128,128]{3,2,1,0:T(8,128)(2,1)S(1)}, bf16[2,8,128,128]{3,2,1,0:T(8,128)(2,1)}, u32[]{:S(2)}, u32[]{:S(2)}) collective-permute-start(bf16[2,8,128,128]{3,2,1,0:T(8,128)(2,1)S(1)} %collective-permute-done.1.refs_2_), channel_id=1, source_target_pairs={{0,1},{1,0},{2,3},{3,2},{4,5},{5,4},{6,7},{7,6},{8,9},{9,8},{10,11... | collective-permute-start | bytes 1572872 | tf_op jit(solution)/shard_map/ppermute | solution.py:246
  21.9 13.8 %collective-permute-start.3 = (bf16[2,8,128,128]{3,2,1,0:T(8,128)(2,1)S(1)}, bf16[2,8,128,128]{3,2,1,0:T(8,128)(2,1)S(1)}, u32[]{:S(2)}, u32[]{:S(2)}) collective-permute-start(bf16[2,8,128,128]{3,2,1,0:T(8,128)(2,1)S(1)} %bitcast.55), channel_id=1, source_target_pairs={{0,2},{1,3},{2,0},{3,1},{4,6},{5,7},{6,4},{7,5},{8,10},{9,11},{10,... | collective-permute-start | bytes 1572872 | tf_op jit(solution)/shard_map/ppermute | solution.py:246
  23.3 15.1 %collective-permute-start.6 = (bf16[2,8,128,128]{3,2,1,0:T(8,128)(2,1)S(1)}, bf16[2,8,128,128]{3,2,1,0:T(8,128)(2,1)}, u32[]{:S(2)}, u32[]{:S(2)}) collective-permute-start(bf16[2,8,128,128]{3,2,1,0:T(8,128)(2,1)S(1)} %bitcast.56), channel_id=1, source_target_pairs={{0,1},{1,0},{2,3},{3,2},{4,5},{5,4},{6,7},{7,6},{8,9},{9,8},{10,11... | collective-permute-start | bytes 1572872 | tf_op jit(solution)/shard_map/ppermute | solution.py:246
  23.7 0.9 copy-start.10
  35.7 4.5 %copy-start.12 = (bf16[2,8,128,128]{3,2,1,0:T(8,128)(2,1)}, bf16[2,8,128,128]{3,2,1,0:T(8,128)(2,1)S(1)}, u32[]{:S(2)}) copy-start(bf16[2,8,128,128]{3,2,1,0:T(8,128)(2,1)S(1)} %collective-permute-done.3.refs_2_) | copy-start | bytes 1572868
  35.7 2.8 %collective-permute-start.7 = (bf16[2,8,128,128]{3,2,1,0:T(8,128)(2,1)S(1)}, bf16[2,8,128,128]{3,2,1,0:T(8,128)(2,1)S(1)}, u32[]{:S(2)}, u32[]{:S(2)}) collective-permute-start(bf16[2,8,128,128]{3,2,1,0:T(8,128)(2,1)S(1)} %collective-permute-done.3.refs_2_), channel_id=1, source_target_pairs={{0,1},{1,0},{2,3},{3,2},{4,5},{5,4},{6,7},{7,6},{8,9},{9,8},{10,11... | collective-permute-start | bytes 1572872 | tf_op jit(solution)/shard_map/ppermute | solution.py:246
  36.2 21.6 %collective-permute-start.4 = (bf16[2,8,128,128]{3,2,1,0:T(8,128)(2,1)S(1)}, bf16[2,8,128,128]{3,2,1,0:T(8,128)(2,1)S(1)}, u32[]{:S(2)}, u32[]{:S(2)}) collective-permute-start(bf16[2,8,128,128]{3,2,1,0:T(8,128)(2,1)S(1)} %bitcast.51), channel_id=1, source_target_pairs={{0,1},{1,0},{2,3},{3,2},{4,5},{5,4},{6,7},{7,6},{8,9},{9,8},{10,11... | collective-permute-start | bytes 1572872 | tf_op jit(solution)/shard_map/ppermute | solution.py:246
  36.3 19.3 %collective-permute-start.5 = (bf16[2,8,128,128]{3,2,1,0:T(8,128)(2,1)S(1)}, bf16[2,8,128,128]{3,2,1,0:T(8,128)(2,1)S(1)}, u32[]{:S(2)}, u32[]{:S(2)}) collective-permute-start(bf16[2,8,128,128]{3,2,1,0:T(8,128)(2,1)S(1)} %bitcast.52), channel_id=1, source_target_pairs={{0,2},{1,3},{2,0},{3,1},{4,6},{5,7},{6,4},{7,5},{8,10},{9,11},{10,... | collective-permute-start | bytes 1572872 | tf_op jit(solution)/shard_map/ppermute | solution.py:246
  37.7 13.6 %collective-permute-start.8 = (f32[4,8,8,128]{3,2,1,0:T(8,128)}, f32[4,8,8,128]{3,2,1,0:T(8,128)S(1)}, u32[]{:S(2)}, u32[]{:S(2)}) collective-permute-start(f32[4,8,8,128]{3,2,1,0:T(8,128)} %totals.3.refs_11_), channel_id=1, source_target_pairs={{0,1},{1,0},{2,3},{3,2},{4,5},{5,4},{6,7},{7,6},{8,9},{9,8},{10,11... | collective-permute-start | bytes 393224 | tf_op jit(solution)/shard_map/ppermute | solution.py:246
  38.5 13.6 %collective-permute-start.9 = (f32[4,8,8,128]{3,2,1,0:T(8,128)}, f32[4,8,8,128]{3,2,1,0:T(8,128)S(1)}, u32[]{:S(2)}, u32[]{:S(2)}) collective-permute-start(f32[4,8,8,128]{3,2,1,0:T(8,128)} %totals.3.refs_11_), channel_id=1, source_target_pairs={{0,2},{1,3},{2,0},{3,1},{4,6},{5,7},{6,4},{7,5},{8,10},{9,11},{10,... | collective-permute-start | bytes 393224 | tf_op jit(solution)/shard_map/ppermute | solution.py:246
  38.5 1.6 copy-start.14
  38.5 17.0 %collective-permute-start.10 = (f32[4,8,8,128]{3,2,1,0:T(8,128)}, f32[4,8,8,128]{3,2,1,0:T(8,128)S(1)}, u32[]{:S(2)}, u32[]{:S(2)}) collective-permute-start(f32[4,8,8,128]{3,2,1,0:T(8,128)} %totals.3.refs_11_), channel_id=1, source_target_pairs={{0,3},{1,2},{2,1},{3,0},{4,7},{5,6},{6,5},{7,4},{8,11},{9,10},{10,... | collective-permute-start | bytes 393224 | tf_op jit(solution)/shard_map/ppermute | solution.py:246
  51.3 19.3 %copy-start.18 = (f32[4,8,8,128]{3,2,1,0:T(8,128)}, f32[4,8,8,128]{3,2,1,0:T(8,128)S(1)}, u32[]{:S(2)}) copy-start(f32[4,8,8,128]{3,2,1,0:T(8,128)S(1)} %collective-permute-done.8.refs_12_) | copy-start | bytes 393220
  52.1 18.5 %copy-start.21 = (f32[4,8,8,128]{3,2,1,0:T(8,128)}, f32[4,8,8,128]{3,2,1,0:T(8,128)S(1)}, u32[]{:S(2)}) copy-start(f32[4,8,8,128]{3,2,1,0:T(8,128)S(1)} %collective-permute-done.9.refs_13_) | copy-start | bytes 393220
  55.5 15.1 %copy-start.23 = (f32[4,8,8,128]{3,2,1,0:T(8,128)}, f32[4,8,8,128]{3,2,1,0:T(8,128)S(1)}, u32[]{:S(2)}) copy-start(f32[4,8,8,128]{3,2,1,0:T(8,128)S(1)} %collective-permute-done.10.refs_14_) | copy-start | bytes 393220
  55.5 2.3 %copy-start.9 = (bf16[2,8,128,128]{3,2,1,0:T(8,128)(2,1)}, bf16[2,8,128,128]{3,2,1,0:T(8,128)(2,1)S(1)}, u32[]{:S(2)}) copy-start(bf16[2,8,128,128]{3,2,1,0:T(8,128)(2,1)S(1)} %collective-permute-done.5.refs_2_) | copy-start | bytes 1572868
  55.5 2.3 %collective-permute-start.11 = (bf16[2,8,128,128]{3,2,1,0:T(8,128)(2,1)S(1)}, bf16[2,8,128,128]{3,2,1,0:T(8,128)(2,1)S(1)}, u32[]{:S(2)}, u32[]{:S(2)}) collective-permute-start(bf16[2,8,128,128]{3,2,1,0:T(8,128)(2,1)S(1)} %collective-permute-done.5.refs_2_), channel_id=1, source_target_pairs={{0,1},{1,0},{2,3},{3,2},{4,5},{5,4},{6,7},{7,6},{8,9},{9,8},{10,11... | collective-permute-start | bytes 1572872 | tf_op jit(solution)/shard_map/ppermute | solution.py:246
  55.6 15.0 %collective-permute-start.12 = (f32[4,8,8,128]{3,2,1,0:T(8,128)}, f32[4,8,8,128]{3,2,1,0:T(8,128)S(1)}, u32[]{:S(2)}, u32[]{:S(2)}) collective-permute-start(f32[4,8,8,128]{3,2,1,0:T(8,128)} %totals.4.refs_11_), channel_id=1, source_target_pairs={{0,1},{1,0},{2,3},{3,2},{4,5},{5,4},{6,7},{7,6},{8,9},{9,8},{10,11... | collective-permute-start | bytes 393224 | tf_op jit(solution)/shard_map/ppermute | solution.py:246
  56.1 14.5 %collective-permute-start.13 = (f32[4,8,8,128]{3,2,1,0:T(8,128)}, f32[4,8,8,128]{3,2,1,0:T(8,128)S(1)}, u32[]{:S(2)}, u32[]{:S(2)}) collective-permute-start(f32[4,8,8,128]{3,2,1,0:T(8,128)} %totals.4.refs_11_), channel_id=1, source_target_pairs={{0,2},{1,3},{2,0},{3,1},{4,6},{5,7},{6,4},{7,5},{8,10},{9,11},{10,... | collective-permute-start | bytes 393224 | tf_op jit(solution)/shard_map/ppermute | solution.py:246
  57.6 13.1 %collective-permute-start.14 = (f32[4,8,8,128]{3,2,1,0:T(8,128)}, f32[4,8,8,128]{3,2,1,0:T(8,128)S(1)}, u32[]{:S(2)}, u32[]{:S(2)}) collective-permute-start(f32[4,8,8,128]{3,2,1,0:T(8,128)} %totals.4.refs_11_), channel_id=1, source_target_pairs={{0,3},{1,2},{2,1},{3,0},{4,7},{5,6},{6,5},{7,4},{8,11},{9,10},{10,... | collective-permute-start | bytes 393224 | tf_op jit(solution)/shard_map/ppermute | solution.py:246
  58.7 0.8 copy-start.13
  70.6 23.1 %copy-start.19 = (f32[4,8,8,128]{3,2,1,0:T(8,128)}, f32[4,8,8,128]{3,2,1,0:T(8,128)S(1)}, u32[]{:S(2)}) copy-start(f32[4,8,8,128]{3,2,1,0:T(8,128)S(1)} %collective-permute-done.12.refs_12_) | copy-start | bytes 393220
  70.7 23.1 %copy-start.20 = (f32[4,8,8,128]{3,2,1,0:T(8,128)}, f32[4,8,8,128]{3,2,1,0:T(8,128)S(1)}, u32[]{:S(2)}) copy-start(f32[4,8,8,128]{3,2,1,0:T(8,128)S(1)} %collective-permute-done.13.refs_13_) | copy-start | bytes 393220
  70.7 23.1 %copy-start.22 = (f32[4,8,8,128]{3,2,1,0:T(8,128)}, f32[4,8,8,128]{3,2,1,0:T(8,128)S(1)}, u32[]{:S(2)}) copy-start(f32[4,8,8,128]{3,2,1,0:T(8,128)S(1)} %collective-permute-done.14.refs_14_) | copy-start | bytes 393220
  70.7 23.1 %collective-permute-start.15 = (f32[4,8,8,128]{3,2,1,0:T(8,128)}, f32[4,8,8,128]{3,2,1,0:T(8,128)S(1)}, u32[]{:S(2)}, u32[]{:S(2)}) collective-permute-start(f32[4,8,8,128]{3,2,1,0:T(8,128)} %totals.5.refs_11_), channel_id=1, source_target_pairs={{0,1},{1,0},{2,3},{3,2},{4,5},{5,4},{6,7},{7,6},{8,9},{9,8},{10,11... | collective-permute-start | bytes 393224 | tf_op jit(solution)/shard_map/ppermute | solution.py:246
  71.1 22.7 %collective-permute-start.16 = (f32[4,8,8,128]{3,2,1,0:T(8,128)}, f32[4,8,8,128]{3,2,1,0:T(8,128)S(1)}, u32[]{:S(2)}, u32[]{:S(2)}) collective-permute-start(f32[4,8,8,128]{3,2,1,0:T(8,128)} %totals.5.refs_11_), channel_id=1, source_target_pairs={{0,2},{1,3},{2,0},{3,1},{4,6},{5,7},{6,4},{7,5},{8,10},{9,11},{10,... | collective-permute-start | bytes 393224 | tf_op jit(solution)/shard_map/ppermute | solution.py:246
  72.5 21.3 %collective-permute-start.17 = (f32[4,8,8,128]{3,2,1,0:T(8,128)}, f32[4,8,8,128]{3,2,1,0:T(8,128)S(1)}, u32[]{:S(2)}, u32[]{:S(2)}) collective-permute-start(f32[4,8,8,128]{3,2,1,0:T(8,128)} %totals.5.refs_11_), channel_id=1, source_target_pairs={{0,3},{1,2},{2,1},{3,0},{4,7},{5,6},{6,5},{7,4},{8,11},{9,10},{10,... | collective-permute-start | bytes 393224 | tf_op jit(solution)/shard_map/ppermute | solution.py:246
  93.8 31.3 %copy-start.15 = (f32[4,8,8,128]{3,2,1,0:T(8,128)}, f32[4,8,8,128]{3,2,1,0:T(8,128)S(1)}, u32[]{:S(2)}) copy-start(f32[4,8,8,128]{3,2,1,0:T(8,128)S(1)} %collective-permute-done.15.refs_12_) | copy-start | bytes 393220
  94.6 30.6 %collective-permute-start.18 = (bf16[2,8,128,128]{3,2,1,0:T(8,128)(2,1)}, bf16[2,8,128,128]{3,2,1,0:T(8,128)(2,1)S(1)}, u32[]{:S(2)}, u32[]{:S(2)}) collective-permute-start(bf16[2,8,128,128]{3,2,1,0:T(8,128)(2,1)} %get-tuple-element.94), channel_id=1, source_target_pairs={{0,1},{1,0},{2,3},{3,2},{4,5},{5,4},{6,7},{7,6},{8,9},{9,8},{10,11... | collective-permute-start | bytes 1572872 | tf_op jit(solution)/shard_map/ppermute | solution.py:246
  94.6 33.8 %all-to-all-start = ((bf16[32,16,1536]{2,1,0:T(8,128)(2,1)}), bf16[32,16,1536]{2,1,0:T(8,128)(2,1)S(1)}, u32[]{:S(2)}, u32[]{:S(2)}) async-start(bf16[32,16,1536]{2,1,0:T(8,128)(2,1)} %bitcast.45), calls=%async_computation | async-start | bytes 3145728 | tf_op jit(solution)/shard_map/all_to_all | solution.py:296
  104.7 20.4 %copy-start.7 = (bf16[2,8,128,128]{3,2,1,0:T(8,128)(2,1)S(1)}, bf16[2,8,128,128]{3,2,1,0:T(8,128)(2,1)}, u32[]{:S(2)}) copy-start(bf16[2,8,128,128]{3,2,1,0:T(8,128)(2,1)} %get-tuple-element.93) | copy-start | bytes 1572868
  128.4 31.1 %collective-permute-start.19 = (bf16[8,128,128]{2,1,0:T(8,128)(2,1)S(1)}, bf16[8,128,128]{2,1,0:T(8,128)(2,1)}, u32[]{:S(2)}, u32[]{:S(2)}) collective-permute-start(bf16[8,128,128]{2,1,0:T(8,128)(2,1)S(1)} %fusion.2), channel_id=1, source_target_pairs={{0,2},{1,3},{2,0},{3,1},{4,6},{5,7},{6,4},{7,5},{8,10},{9,11},{10,... | collective-permute-start | bytes 786440 | tf_op jit(solution)/shard_map/ppermute | solution.py:246
  129.2 31.4 %collective-permute-start.20 = (bf16[2,8,128,128]{3,2,1,0:T(8,128)(2,1)}, bf16[2,8,128,128]{3,2,1,0:T(8,128)(2,1)}, u32[]{:S(2)}, u32[]{:S(2)}) collective-permute-start(bf16[2,8,128,128]{3,2,1,0:T(8,128)(2,1)} %get-tuple-element.108), channel_id=1, source_target_pairs={{0,1},{1,0},{2,3},{3,2},{4,5},{5,4},{6,7},{7,6},{8,9},{9,8},{10,11... | collective-permute-start | bytes 1572872 | tf_op jit(solution)/shard_map/ppermute | solution.py:246
  131.1 32.4 %all-to-all-start.1 = ((bf16[32,16,1536]{2,1,0:T(8,128)(2,1)}), bf16[32,16,1536]{2,1,0:T(8,128)(2,1)S(1)}, u32[]{:S(2)}, u32[]{:S(2)}) async-start(bf16[32,16,1536]{2,1,0:T(8,128)(2,1)} %bitcast.44), calls=%async_computation.1 | async-start | bytes 3145728 | tf_op jit(solution)/shard_map/all_to_all | solution.py:296
  138.1 21.4 %copy-start.1 = (f32[8,128,128]{2,1,0:T(8,128)S(1)}, f32[8,128,128]{2,1,0:T(8,128)}, u32[]{:S(2)}) copy-start(f32[8,128,128]{2,1,0:T(8,128)} %slice_bitcast_fusion.2) | copy-start | bytes 1572868
  163.5 2.1 %collective-permute-start.22 = (bf16[2,8,128,128]{3,2,1,0:T(8,128)(2,1)}, bf16[2,8,128,128]{3,2,1,0:T(8,128)(2,1)S(1)}, u32[]{:S(2)}, u32[]{:S(2)}) collective-permute-start(bf16[2,8,128,128]{3,2,1,0:T(8,128)(2,1)} %get-tuple-element.123), channel_id=1, source_target_pairs={{0,1},{1,0},{2,3},{3,2},{4,5},{5,4},{6,7},{7,6},{8,9},{9,8},{10,11... | collective-permute-start | bytes 1572872 | tf_op jit(solution)/shard_map/ppermute | solution.py:246
  168.4 40.6 %all-to-all-start.2 = ((bf16[32,16,1536]{2,1,0:T(8,128)(2,1)}), bf16[32,16,1536]{2,1,0:T(8,128)(2,1)}, u32[]{:S(2)}, u32[]{:S(2)}) async-start(bf16[32,16,1536]{2,1,0:T(8,128)(2,1)} %bitcast.43), calls=%async_computation.2 | async-start | bytes 3145728 | tf_op jit(solution)/shard_map/all_to_all | solution.py:296
  177.9 24.4 %copy-start.2 = (f32[8,128,128]{2,1,0:T(8,128)S(1)}, f32[8,128,128]{2,1,0:T(8,128)}, u32[]{:S(2)}) copy-start(f32[8,128,128]{2,1,0:T(8,128)} %slice_bitcast_fusion.1) | copy-start | bytes 1572868
  177.9 29.9 %copy-start.3 = (f32[8,128,128]{2,1,0:T(8,128)S(1)}, f32[8,128,128]{2,1,0:T(8,128)}, u32[]{:S(2)}) copy-start(f32[8,128,128]{2,1,0:T(8,128)} %slice_bitcast_fusion) | copy-start | bytes 1572868
  178.0 24.4 %collective-permute-start.21 = (bf16[8,128,128]{2,1,0:T(8,128)(2,1)}, bf16[8,128,128]{2,1,0:T(8,128)(2,1)S(1)}, u32[]{:S(2)}, u32[]{:S(2)}) collective-permute-start(bf16[8,128,128]{2,1,0:T(8,128)(2,1)} %fusion.3), channel_id=1, source_target_pairs={{0,2},{1,3},{2,0},{3,1},{4,6},{5,7},{6,4},{7,5},{8,10},{9,11},{10,... | collective-permute-start | bytes 786440 | tf_op jit(solution)/shard_map/ppermute | solution.py:246
  178.3 29.6 %collective-permute-start.23 = (bf16[8,128,128]{2,1,0:T(8,128)(2,1)}, bf16[8,128,128]{2,1,0:T(8,128)(2,1)S(1)}, u32[]{:S(2)}, u32[]{:S(2)}) collective-permute-start(bf16[8,128,128]{2,1,0:T(8,128)(2,1)} %fusion.4), channel_id=1, source_target_pairs={{0,2},{1,3},{2,0},{3,1},{4,6},{5,7},{6,4},{7,5},{8,10},{9,11},{10,... | collective-permute-start | bytes 786440 | tf_op jit(solution)/shard_map/ppermute | solution.py:246
  (3 other events, 2.2 us)
where the time goes:
time: 213 us; the launch traced here: 211 us
  Pallas kernels  95.3 us (45%)
  starting transfers between devices  46.1 us (22%)
  waiting for transfers between devices  38.1 us (18%)
  local copies, waits for them, and re-layouts  17.4 us (8%)
  other arithmetic  12.9 us (6%)
    pallas_call x3, Pallas kernels, grads(): pl.pallas_call(functools.partial(grads_kernel, not carried, last), grid_s...  61.9 us
    ppermute x24, waiting for transfers between devices, partner(): return lax.ppermute(x, 'cols', [(c, c ^ distance) for c in range(4)])  35.8 us
    pallas_call x3, Pallas kernels, totals(): pl.pallas_call(totals_kernel, grid_spec=pltpu.PrefetchScalarGridSpec(num_...  33.4 us
    all_to_all x3, starting transfers between devices, swap_bias(): return lax.all_to_all(db, 'rows', 0, 0, tiled=True)  26.7 us
    ppermute x24, starting transfers between devices, partner(): return lax.ppermute(x, 'cols', [(c, c ^ distance) for c in range(4)])  19.4 us
    slice x1, local copies, waits for them, and re-layouts, per_device(): pair_bias[:, h]  6.84 us
  transfers between devices with their start and end apart: 27, of which 7 were waited for; matrix products, arithmetic and copies ran while one was open for 9% of the time, Pallas kernels for 45%

commit v1 on v0

v1 whole, which is shorter than its diff:
```python
import functools

import jax
import jax.numpy as jnp
from jax import lax
from jax.experimental import pallas as pl
from jax.experimental.pallas import tpu as pltpu
from jax.sharding import PartitionSpec as P

HEADS = 4
HEAD_DIM = 32
CH = HEADS * HEAD_DIM
SCALE = HEAD_DIM**-0.5
LOG2E = 1.4426950408889634
CHUNKS = 2
TILE = 256
VMEM = 60 * 2**20
NT = (((1,), (1,)), ((), ()))
F32 = jnp.float32
BF16 = jnp.bfloat16


def only_head(x, h):
    lane = lax.broadcasted_iota(jnp.int32, (1, x.shape[1]), 1)
    hit = (lane >= h * HEAD_DIM) & (lane < (h + 1) * HEAD_DIM)
    return x * jnp.where(hit, 1.0, 0.0).astype(BF16)


def joined(parts, which):
    return jnp.concatenate([part[which, 0] for part in parts], axis=0)


def bias_block(parts):
    return jnp.concatenate([part[0, 0] for part in parts], axis=0).astype(F32) * LOG2E


def totals_kernel(col_ref, *refs):
    n = (len(refs) - 6) // 2
    parts, biases, (k_ref, v_ref, gate_ref, out_ref, e_ref, bias_ref) = refs[:n], refs[n : 2 * n], refs[2 * n :]
    q, g = joined(parts, 0), joined(parts, 1)
    k = k_ref[0]
    key_len = k.shape[0]

    @pl.when(pl.program_id(0) == 0)
    def start():
        bias = bias_block(biases)
        gate = jnp.concatenate([gate_ref[...]] * (q.shape[0] // CH), axis=1)
        for h in range(HEADS):
            bias_ref[h] = bias[:, h * key_len : (h + 1) * key_len].T + gate

    for h in range(HEADS):
        s = lax.dot_general(k, only_head(q, h), NT, preferred_element_type=F32)
        e_ref[h] = jnp.exp2(s * (SCALE * LOG2E) + bias_ref[h]).astype(BF16)
    gt = g.T.astype(F32)
    vt = v_ref[0].T
    ones = jnp.ones((16, key_len), BF16)
    for h in range(HEADS):
        rows = slice(h * HEAD_DIM, (h + 1) * HEAD_DIM)
        o = jnp.dot(jnp.concatenate([vt[rows], ones], axis=0), e_ref[h], preferred_element_type=F32)
        total = o[HEAD_DIM : HEAD_DIM + 1]
        weighted = jnp.sum(o[:HEAD_DIM] * gt[rows], axis=0, keepdims=True)
        for u in range(n):
            at = slice(u * (q.shape[0] // n), (u + 1) * (q.shape[0] // n))
            out_ref[col_ref[0] ^ u, 0, h : h + 1] = total[:, at]
            out_ref[col_ref[0] ^ u, 0, HEADS + h : HEADS + h + 1] = weighted[:, at]


def part_specs(part_len, bias, chunk):
    width = bias.shape[-1]
    data = [pl.BlockSpec((2, 1, part_len, CH), lambda i, col: (0, i, 0, 0))] * 4
    return data + [
        pl.BlockSpec((1, 1, part_len, width), lambda i, col, u=u: (chunk, col[0] ^ u, 0, 0)) for u in range(4)
    ]


def totals(col, parts, bias, chunk, keys, values, key_gate):
    rows, key_len, _ = keys.shape
    part_len = parts[0].shape[2]
    n = len(parts)
    count = n * part_len
    per_row = lambda i, col: (i, 0, 0)
    work = rows * count * HEADS * key_len
    return pl.pallas_call(
        totals_kernel,
        grid_spec=pltpu.PrefetchScalarGridSpec(
            num_scalar_prefetch=1,
            grid=(rows,),
            in_specs=part_specs(part_len, bias, chunk)
            + [
                pl.BlockSpec((1, key_len, CH), per_row),
                pl.BlockSpec((1, key_len, CH), per_row),
                pl.BlockSpec((key_len, CH), lambda i, col: (0, 0)),
            ],
            out_specs=pl.BlockSpec((n, 1, 2 * HEADS, part_len), lambda i, col: (0, i, 0, 0)),
            scratch_shapes=[pltpu.VMEM((HEADS, key_len, count), BF16), pltpu.VMEM((HEADS, key_len, count), F32)],
        ),
        out_shape=jax.ShapeDtypeStruct((n, rows, 2 * HEADS, part_len), F32),
        compiler_params=pltpu.CompilerParams(vmem_limit_bytes=VMEM),
        cost_estimate=pl.CostEstimate(flops=work * 512 * 3, bytes_accessed=2**20, transcendentals=work),
        name="totals",
    )(col, *parts, *[bias] * n, keys, values, key_gate)


def split(x):
    a = x.astype(BF16)
    rest = x - a.astype(F32)
    b = rest.astype(BF16)
    return [y.astype(F32) for y in (a, b, (rest - b.astype(F32)).astype(BF16))]


def load_keys(ref, x, column=None):
    key_len = x.shape[0]
    for h in range(HEADS):
        rows = slice(h * key_len, (h + 1) * key_len)
        if column is None:
            ref[rows, :CH] = only_head(x, h)
        else:
            lane = lax.broadcasted_iota(jnp.int32, (key_len, CH), 1)
            hit = (lane < 6 * HEADS) & (lane % (2 * HEADS) == column + h)
            ref[rows, CH:] = jnp.where(hit, -1.0, 0.0).astype(BF16)


def with_extra(q, g, stats, col):
    stat = [sum(ref[col ^ u, 0] for ref in stats[1:]) + stats[0][col ^ u, 0] for u in range(4)]
    stat = jnp.concatenate(stat, axis=1)
    total = stat[:HEADS]
    level = jnp.log(total) * (1.0 / SCALE)
    delta = stat[HEADS:] / total
    pieces = split(jnp.concatenate([level, delta], axis=0))
    extra = jnp.concatenate(pieces + [jnp.zeros((CH - 6 * HEADS, q.shape[0]), F32)], axis=0).T.astype(BF16)
    return jnp.concatenate([q, extra], axis=1), jnp.concatenate([g, extra], axis=1)


def chances(qx, gx, kx_ref, vx_ref, bias_ref, at):
    s = lax.dot_general(qx, kx_ref[at], NT, preferred_element_type=F32)
    t = lax.dot_general(gx, vx_ref[at], NT, preferred_element_type=F32)
    p = jnp.exp2(s * (SCALE * LOG2E) + bias_ref[:, at])
    return p, p * t


def prepare(biases, gate_ref, sum_ref, bias_ref, kx_ref, vx_ref, k, v):
    @pl.when(pl.program_id(0) == 0)
    def start():
        sum_ref[...] = jnp.zeros(sum_ref.shape, F32)
        bias_ref[...] = bias_block(biases) + jnp.concatenate([gate_ref[:1]] * HEADS, axis=1)
        load_keys(kx_ref, k, 0)
        load_keys(vx_ref, v, HEADS)

    load_keys(kx_ref, k)
    load_keys(vx_ref, v)


def store_bias(col, sum_ref, db_ref):
    @pl.when(pl.program_id(0) == pl.num_programs(0) - 1)
    def finish():
        part_len = db_ref.shape[1]
        for u in range(4):
            db_ref[col ^ u] = sum_ref[u * part_len : (u + 1) * part_len].astype(BF16)


def store_queries(dq, dq_refs):
    dq = (dq * SCALE).astype(BF16)
    part_len = dq.shape[0] // 4
    for u in range(4):
        dq_refs[u % 2][u // 2, 0] = dq[u * part_len : (u + 1) * part_len]


def grads_kernel(col_ref, *refs):
    parts, biases, refs = refs[:4], refs[4:8], refs[8:]
    k_ref, v_ref, gate_ref, *refs = refs
    stats, dq_refs, refs = refs[:4], refs[4:6], refs[6:]
    dk_ref, dv_ref, db_ref, kx_ref, vx_ref, sum_ref, p_ref, ds_ref, bias_ref = refs
    col = col_ref[0]
    q, g = joined(parts, 0), joined(parts, 1)
    key_len = k_ref.shape[1]
    prepare(biases, gate_ref, sum_ref, bias_ref, kx_ref, vx_ref, k_ref[0], v_ref[0])
    qx, gx = with_extra(q, g, stats, col)
    qt, gt = q.T, g.T
    dq = jnp.zeros((q.shape[0], CH), F32)
    for n in range(HEADS * key_len // TILE):
        at = slice(n * TILE, (n + 1) * TILE)
        p, ds = chances(qx, gx, kx_ref, vx_ref, bias_ref, at)
        sum_ref[:, at] += ds
        low = ds.astype(BF16)
        p_ref[:, at] = p.astype(BF16)
        ds_ref[:, at] = low
        dq = dq + jnp.dot(low, kx_ref[at, :CH], preferred_element_type=F32)
    store_queries(dq, dq_refs)
    for h in range(HEADS):
        rows, at = slice(h * HEAD_DIM, (h + 1) * HEAD_DIM), slice(h * key_len, (h + 1) * key_len)
        dv_ref[0, rows] = jnp.dot(gt[rows], p_ref[:, at], preferred_element_type=F32)
        dk_ref[0, rows] = jnp.dot(qt[rows], ds_ref[:, at], preferred_element_type=F32)
    store_bias(col, sum_ref, db_ref)


def chances_kernel(col_ref, *refs):
    parts, biases, refs = refs[:4], refs[4:8], refs[8:]
    k_ref, v_ref, gate_ref, *refs = refs
    stats, refs = refs[:4], refs[4:]
    p_ref, ds_ref, db_ref, kx_ref, vx_ref, sum_ref, bias_ref = refs
    col = col_ref[0]
    prepare(biases, gate_ref, sum_ref, bias_ref, kx_ref, vx_ref, k_ref[0], v_ref[0])
    qx, gx = with_extra(joined(parts, 0), joined(parts, 1), stats, col)
    for n in range(HEADS * k_ref.shape[1] // TILE):
        at = slice(n * TILE, (n + 1) * TILE)
        p, ds = chances(qx, gx, kx_ref, vx_ref, bias_ref, at)
        sum_ref[:, at] += ds
        p_ref[0, :, at] = p.astype(BF16)
        ds_ref[0, :, at] = ds.astype(BF16)
    store_bias(col, sum_ref, db_ref)


def products_kernel(*refs):
    parts, refs = refs[:4], refs[4:]
    k_ref, p_ref, ds_ref, dk_in, dv_in, *refs = refs
    dq_refs, (dk_out, dv_out, kx_ref, dk_ref, dv_ref) = refs[:2], refs[2:]
    q, g = joined(parts, 0), joined(parts, 1)
    key_len = k_ref.shape[1]
    load_keys(kx_ref, k_ref[0])
    store_queries(jnp.dot(ds_ref[0], kx_ref[...], preferred_element_type=F32), dq_refs)
    qt, gt = q.T, g.T
    for h in range(HEADS):
        rows, at = slice(h * HEAD_DIM, (h + 1) * HEAD_DIM), slice(h * key_len, (h + 1) * key_len)
        dv_ref[rows] = jnp.dot(gt[rows], p_ref[0, :, at], preferred_element_type=F32) + dv_in[0, rows]
        dk = jnp.dot(qt[rows], ds_ref[0, :, at], preferred_element_type=F32)
        dk_ref[rows] = (dk + dk_in[0, rows]) * SCALE
    dv_out[0] = dv_ref[...].T.astype(BF16)
    dk_out[0] = dk_ref[...].T.astype(BF16)


def grads(kind, col, parts, bias, chunk, keys, values, row_gate, stats, carried=()):
    rows, key_len, _ = keys.shape
    part_len = parts[0].shape[2]
    count, width = 4 * part_len, HEADS * key_len
    per_row = lambda i, *col: (i, 0, 0)
    whole = lambda i, *col: (0, 0)
    data = pl.BlockSpec((1, key_len, CH), per_row)
    side = pl.BlockSpec((1, CH, key_len), per_row)
    side_shape = jax.ShapeDtypeStruct((rows, CH, key_len), F32)
    data_shape = jax.ShapeDtypeStruct(keys.shape, BF16)
    square = pl.BlockSpec((1, count, width), per_row)
    square_shape = jax.ShapeDtypeStruct((rows, count, width), BF16)
    dq_specs = [pl.BlockSpec((2, 1, part_len, CH), lambda i, *col: (0, i, 0, 0))] * 2
    dq_shapes = [jax.ShapeDtypeStruct((2, rows, part_len, CH), BF16)] * 2
    db_spec = pl.BlockSpec((4, part_len, width), lambda i, *col: (0, 0, 0))
    db_shape = jax.ShapeDtypeStruct((4, part_len, width), BF16)
    stat_specs = [pl.BlockSpec((4, 1, 2 * HEADS, part_len), lambda i, col: (0, i, 0, 0))] * 4
    keys_scratch = pltpu.VMEM((width, 2 * CH), BF16)
    wide, low = pltpu.VMEM((count, width), F32), pltpu.VMEM((count, width), BF16)
    flops = rows * count * width * 512
    if kind == "products":
        return pl.pallas_call(
            products_kernel,
            grid=(rows,),
            in_specs=[pl.BlockSpec((2, 1, part_len, CH), lambda i: (0, i, 0, 0))] * 4
            + [data, square, square, side, side],
            out_specs=dq_specs + [data, data],
            out_shape=dq_shapes + [data_shape, data_shape],
            scratch_shapes=[pltpu.VMEM((width, CH), BF16), pltpu.VMEM((CH, key_len), F32), pltpu.VMEM((CH, key_len), F32)],
            compiler_params=pltpu.CompilerParams(vmem_limit_bytes=VMEM),
            cost_estimate=pl.CostEstimate(flops=flops * 3, bytes_accessed=2**20, transcendentals=0),
            name="products",
        )(*parts, keys, *carried)
    in_specs = part_specs(part_len, bias, chunk) + [data, data, pl.BlockSpec((8, key_len), whole)] + stat_specs
    if kind == "chances":
        out_specs, out_shape = [square, square, db_spec], [square_shape, square_shape, db_shape]
        scratch = [keys_scratch, keys_scratch, wide, wide]
    else:
        out_specs = dq_specs + [side, side, db_spec]
        out_shape = dq_shapes + [side_shape, side_shape, db_shape]
        scratch = [keys_scratch, keys_scratch, wide, low, low, wide]
    return pl.pallas_call(
        chances_kernel if kind == "chances" else grads_kernel,
        grid_spec=pltpu.PrefetchScalarGridSpec(
            num_scalar_prefetch=1, grid=(rows,), in_specs=in_specs, out_specs=out_specs, scratch_shapes=scratch
        ),
        out_shape=out_shape,
        compiler_params=pltpu.CompilerParams(vmem_limit_bytes=VMEM),
        cost_estimate=pl.CostEstimate(flops=flops * (4 if kind == "chances" else 6), bytes_accessed=2**20, transcendentals=0),
        name=kind,
    )(col, *parts, *[bias] * 4, keys, values, row_gate, *stats)


def partner(x, distance):
    return lax.ppermute(x, "cols", [(c, c ^ distance) for c in range(4)])


def per_device(queries, keys, values, out_grad, pair_bias, token_mask, span_index):
    rows, key_len, _ = keys.shape
    col = lax.axis_index("cols")
    owners = 8
    span = key_len // owners
    step = span // CHUNKS
    part_len = owners * step
    count = 4 * part_len
    width = HEADS * key_len

    row_keep = lax.dynamic_slice_in_dim(token_mask, span_index[0] * rows, rows)
    masked = out_grad * row_keep.astype(BF16)[:, None, None]
    pairs = jnp.stack([queries, masked]).reshape(2, rows, owners, CHUNKS, step, CH)

    key_keep = lax.dynamic_slice_in_dim(token_mask, col * key_len, key_len) > 0
    gate = jnp.where(key_keep, F32(0.0), F32(-1e30))
    key_gate = jnp.broadcast_to(gate[:, None], (key_len, CH))
    row_gate = jnp.broadcast_to(gate[None, :], (8, key_len))
    bias = jnp.concatenate([pair_bias[:, h] for h in range(HEADS)], axis=1)
    bias = bias.reshape(4 * owners, CHUNKS, step, width).swapaxes(0, 1).reshape(CHUNKS, 4, part_len, width)
    col_id = col.astype(jnp.int32).reshape(1)

    tie = lax.optimization_barrier
    owns = [pairs[:, :, :, b].reshape(2, rows, part_len, CH) for b in range(CHUNKS)]

    def spread(own, far):
        return [own, partner(own, 1), far, partner(far, 1)]

    def call_totals(b):
        return totals(col_id, parts[b], bias, b, keys, values, key_gate)

    def all_stats(stat):
        return [stat] + [partner(stat, distance) for distance in (1, 2, 3)]

    def call_grads(kind, b, stats, carried=()):
        return grads(kind, col_id, parts[b], bias, b, keys, values, row_gate, stats, carried)

    def near_queries(dq):
        pair = dq[0].astype(F32) + partner(dq[1], 1).astype(F32)
        return pair[0], pair[1].astype(BF16)

    def far_queries(pair):
        return (pair[0] + partner(pair[1], 2).astype(F32)).astype(BF16)

    def swap_bias(db):
        return lax.all_to_all(db.reshape(32, step, width), "rows", 0, 0, tiled=True)

    def summed(terms):
        return jnp.sum(terms.astype(F32), axis=0)

    far0, bias = tie((partner(owns[0], 2), bias))
    far0, owns[1] = tie((far0, owns[1]))
    far1 = partner(owns[1], 2)
    parts = [spread(owns[0], far0), None]
    t0 = call_totals(0)
    far1, t0 = tie((far1, t0))
    parts[1] = spread(owns[1], far1)
    t1 = call_totals(1)
    s0, t1 = tie((all_stats(t0), t1))
    p, ds, db0 = call_grads("chances", 0, s0)
    db0, s1 = tie((db0, all_stats(t1)))
    *dq1, dk, dv, db1 = call_grads("grads", 1, s1)
    db0, dq1, db1 = tie((swap_bias(db0), dq1, db1))
    db1 = swap_bias(db1)
    n1, p = tie((near_queries(dq1), p))
    *dq0, key_grad, value_grad = call_grads("products", 0, (), (p, ds, dk, dv))
    q1, dq0 = tie((far_queries(n1), dq0))
    n0 = near_queries(dq0)
    queries_out = [far_queries(n0), q1]
    bias_out = [summed(db0), summed(db1)]
    query_grad = jnp.stack(queries_out).reshape(CHUNKS, rows, owners, step, CH)
    query_grad = query_grad.transpose(1, 2, 0, 3, 4).reshape(rows, key_len, CH)
    bias_grad = jnp.concatenate(bias_out, axis=0).reshape(span, HEADS, key_len)
    return (query_grad, key_grad, value_grad, bias_grad)


def solution(mesh):
    return jax.shard_map(
        per_device,
        mesh=mesh,
        in_specs=(
            P("rows", "cols", None),
            P("rows", "cols", None),
            P("rows", "cols", None),
            P("rows", "cols", None),
            P(None, None, "cols"),
            P(),
            P("rows"),
        ),
        out_specs=(
            P("rows", "cols", None),
            P("rows", "cols", None),
            P("rows", "cols", None),
            P("rows", None, "cols"),
        ),
        check_vma=False,
    )
```

time: 213 us -> 192 us (0.901)
  starting transfers between devices: 46.1 us -> 31.6 us
  waiting for transfers between devices: 38.1 us -> 32.5 us
  Pallas kernels: 95.3 us -> 99.7 us
    all_to_all x3 -> x2, starting transfers between devices: 26.7 us -> 16.4 us  [swap_bias(): return lax.all_to_all(db.reshape(32, step, width), 'rows', 0, 0, tiled=True)]
    pallas_call x3, Pallas kernels: 61.9 us -> 70.5 us  [the longest x2 50.5 us: grads(): pl.pallas_call(chances_kernel if kind == 'chances' else grads_kernel, gri...]
    ppermute x24 -> x16, waiting for transfers between devices: 35.8 us -> 29.1 us  [partner(): return lax.ppermute(x, 'cols', [(c, c ^ distance) for c in range(4)])]
    ppermute x24 -> x16, starting transfers between devices: 19.4 us -> 15.1 us  [partner(): return lax.ppermute(x, 'cols', [(c, c ^ distance) for c in range(4)])]
    pallas_call x3 -> x2, Pallas kernels: 33.4 us -> 29.2 us  [totals(): pl.pallas_call(totals_kernel, grid_spec=pltpu.PrefetchScalarGridSpec(num_...]
    concatenate x2 -> x1, other arithmetic: 2.54 us -> 0.02 us  [per_device(): bias_grad = jnp.concatenate(bias_out, axis=0).reshape(span, HEADS, key_len)]
    squeeze x3 -> x1, local copies, waits for them, and re-layouts: 2.51 us -> 0.05 us  [near_queries(): return (pair[0], pair[1].astype(BF16))]
    transpose x0 -> x1, local copies, waits for them, and re-layouts: none -> 2.45 us  [per_device(): bias.reshape(4 * owners, CHUNKS, step, width).swapaxes(0, 1)]
  transfers between devices with their start and end apart: 27 -> 18, of which waited for: 7 -> 6; matrix products, arithmetic and copies ran while one was open for 9% -> 10% of each run, Pallas kernels for 45% -> 52%
where the time goes in v1:
time: 192 us
  Pallas kernels  99.7 us (52%)
  waiting for transfers between devices  32.5 us (17%)
  starting transfers between devices  31.6 us (16%)
  local copies, waits for them, and re-layouts  15.3 us (8%)
  other arithmetic  10.8 us (6%)
    pallas_call x2, Pallas kernels, grads(): pl.pallas_call(chances_kernel if kind == 'chances' else grads_kernel, gri...  50.5 us
    pallas_call x2, Pallas kernels, totals(): pl.pallas_call(totals_kernel, grid_spec=pltpu.PrefetchScalarGridSpec(num_...  29.2 us
    ppermute x16, waiting for transfers between devices, partner(): return lax.ppermute(x, 'cols', [(c, c ^ distance) for c in range(4)])  29.1 us
    pallas_call x1, Pallas kernels, grads(): pl.pallas_call(products_kernel, grid=(rows,), in_specs=[pl.BlockSpec((2,...  20 us
    all_to_all x2, starting transfers between devices, swap_bias(): return lax.all_to_all(db.reshape(32, step, width), 'rows', 0, 0, tiled=True)  16.4 us
    ppermute x16, starting transfers between devices, partner(): return lax.ppermute(x, 'cols', [(c, c ^ distance) for c in range(4)])  15.1 us
    slice x1, local copies, waits for them, and re-layouts, per_device(): bias = jnp.concatenate([pair_bias[:, h] for h in range(HEADS)], axis=1)  6.84 us
  transfers between devices with their start and end apart: 18, of which 6 were waited for; matrix products, arithmetic and copies ran while one was open for 10% of the time, Pallas kernels for 52%

profile of v1, /device:TPU:1, one launch (start us, length us, event | category | flops | bytes accessed | tf_op | source)
XLA Modules:
  0.0 191.5 jit_solution(6237855294936214897)
XLA Ops:
  1.3 0.8 dynamic-slice_convert_fusion
  2.0 1.4 broadcast_multiply_fusion
  3.5 1.5 pad_maximum_fusion
  5.0 2.5 %collective-permute-start.1 = (bf16[2,8,192,128]{3,2,1,0:T(8,128)(2,1)S(1)}, bf16[2,8,192,128]{3,2,1,0:T(8,128)(2,1)S(1)}, u32[]{:S(2)}, u32[]{:S(2)}) collective-permute-start(bf16[2,8,192,128]{3,2,1,0:T(8,128)(2,1)S(1)} %bitcast.63), channel_id=1, source_target_pairs={{0,2},{1,3},{2,0},{3,1},{4,6},{5,7},{6,4},{7,5},{8,10},{9,11},{10,... | collective-permute-start | bytes 2359304 | tf_op jit(solution)/shard_map/ppermute | solution.py:285
  7.5 1.0 collective-permute-start
  8.5 6.8 %fusion.6 = (bf16[1536,1,384]{2,1,0:T(2,128)(2,1)S(1)}, bf16[1536,1,384]{2,1,0:T(2,128)(2,1)S(1)}, bf16[1536,1,384]{2,1,0:T(2,128)(2,1)S(1)}, bf16[1536,1,384]{2,1,0:T(2,128)(2,1)S(1)}) fusion(bf16[1536,4,384]{2,1,0:T(4,128)(2,1)S(1)} %copy-done), kind=kLoop, calls=%fused_computation.24 | loop fusion | bytes 9437184 | tf_op jit(solution)/shard_map/slice | solution.py:306
  15.4 0.2 copy.28
  15.6 0.2 copy.30
  15.8 0.2 copy.29
  16.0 0.2 copy.31
  16.2 0.6 maximum_bitcast_fusion
  16.8 2.5 %copy.24 = bf16[2,32,24,1536]{3,2,1,0:T(8,128)(2,1)} copy(bf16[2,32,24,1536]{3,2,0,1:T(8,128)(2,1)S(1)} %maximum_bitcast_fusion) | data formatting | bytes 9437184 | tf_op jit(solution)/shard_map/transpose | solution.py:307
  19.3 5.5 %collective-permute-done.1.refs_2_ = bf16[2,8,192,128]{3,2,1,0:T(8,128)(2,1)S(1)} collective-permute-done((bf16[2,8,192,128]{3,2,1,0:T(8,128)(2,1)S(1)}, bf16[2,8,192,128]{3,2,1,0:T(8,128)(2,1)S(1)}, u32[]{:S(2)}, u32[]{:S(2)}) %collective-permute-start.1) | collective-permute-done | bytes 786464 | tf_op jit(solution)/shard_map/ppermute | solution.py:285
  24.8 1.3 collective-permute-start.2
  26.0 0.8 fusion.5
  26.8 1.5 collective-permute-start.3
  28.3 0.9 broadcast_in_dim.24.refs_10_
  29.3 14.6 %totals.2.refs_11_ = f32[4,8,8,192]{3,2,1,0:T(8,128)} custom-call(s32[1]{0:T(128)} %bitcast.col_ref, bf16[2,8,192,128]{3,2,1,0:T(8,128)(2,1)} %bitcast.65, bf16[2,8,192,128]{3,2,1,0:T(8,128)(2,1)} %copy-done.7, bf16[2,8,192,128]{3,2,1,0:T(8,128)(2,1)} %copy-done.6, bf16[2,8,192,128]{3,2,1,0:T(8,128)(2,1)} %collective-permute-done.2.refs_3_, ...), custom_call_target="tpu_custom_call" | custom-call | flops 14495514624 | bytes 1048576 | tf_op jit(solution)/shard_map/totals/pallas_call | solution.py:83
  43.9 1.8 collective-permute-done.3.refs_2_
  45.6 1.3 collective-permute-start.8
  46.9 1.3 collective-permute-start.6
  48.4 0.7 collective-permute-start.4
  49.1 0.9 copy-done.8
  50.0 14.6 %totals.3.refs_11_ = f32[4,8,8,192]{3,2,1,0:T(8,128)} custom-call(s32[1]{0:T(128)} %bitcast.col_ref, bf16[2,8,192,128]{3,2,1,0:T(8,128)(2,1)} %bitcast.70, bf16[2,8,192,128]{3,2,1,0:T(8,128)(2,1)} %collective-permute-done.7.refs_1_, bf16[2,8,192,128]{3,2,1,0:T(8,128)(2,1)} %collective-permute-done.3.refs_2_, bf16[2,8,192,128]{3,2,1,0:T(8,128)(2,1)} %copy-done.8, ...), custom_call_target="tpu_custom_call" | custom-call | flops 14495514624 | bytes 1048576 | tf_op jit(solution)/shard_map/totals/pallas_call | solution.py:83
  64.6 1.8 collective-permute-start.11
  66.4 0.5 collective-permute-start.9
  66.8 0.6 broadcast_in_dim.23.refs_10_
  67.4 21.4 %chances.1 = (bf16[8,768,1536]{2,1,0:T(8,128)(2,1)}, bf16[8,768,1536]{2,1,0:T(8,128)(2,1)}, bf16[4,192,1536]{2,1,0:T(8,128)(2,1)}) custom-call(s32[1]{0:T(128)} %bitcast.col_ref, bf16[2,8,192,128]{3,2,1,0:T(8,128)(2,1)} %bitcast.66, bf16[2,8,192,128]{3,2,1,0:T(8,128)(2,1)} %copy-done.7, bf16[2,8,192,128]{3,2,1,0:T(8,128)(2,1)} %copy-done.6, ...), custom_call_target="tpu_custom_call" | custom-call | flops 19327352832 | bytes 1048576 | tf_op jit(solution)/shard_map/chances/pallas_call | solution.py:272
  88.9 0.7 copy-done.9
  89.7 10.1 %all-to-all-start = ((bf16[32,24,1536]{2,1,0:T(8,128)(2,1)}), bf16[32,24,1536]{2,1,0:T(8,128)(2,1)S(1)}, u32[]{:S(2)}, u32[]{:S(2)}) async-start(bf16[32,24,1536]{2,1,0:T(8,128)(2,1)} %bitcast.58), calls=%async_computation | async-start | bytes 4718592 | tf_op jit(solution)/shard_map/all_to_all | solution.py:333
  99.8 29.1 %grads.1 = (bf16[2,8,192,128]{3,2,1,0:T(8,128)(2,1)}, bf16[2,8,192,128]{3,2,1,0:T(8,128)(2,1)}, f32[8,128,384]{2,1,0:T(8,128)}, f32[8,128,384]{2,1,0:T(8,128)}, bf16[4,192,1536]{2,1,0:T(8,128)(2,1)}) custom-call(s32[1]{0:T(128)} %bitcast.col_ref, bf16[2,8,192,128]{3,2,1,0:T(8,128)(2,1)} %bitcast.71, bf16[2,8,192,128]{3,2,1,0:T(8,128)(2,1)} %collective-permute-done.7.refs_1_, ...), custom_call_target="tpu_custom_call" | custom-call | flops 28991029248 | bytes 1048576 | tf_op jit(solution)/shard_map/grads/pallas_call | solution.py:272
  129.0 3.4 %all-to-all-done = bf16[32,24,1536]{2,1,0:T(8,128)(2,1)S(1)} async-done(((bf16[32,24,1536]{2,1,0:T(8,128)(2,1)}), bf16[32,24,1536]{2,1,0:T(8,128)(2,1)S(1)}, u32[]{:S(2)}, u32[]{:S(2)}) %all-to-all-start) | async-done | bytes 2359328 | tf_op jit(solution)/shard_map/all_to_all | solution.py:333
  132.4 1.0 collective-permute-start.12
  133.4 6.3 %all-to-all-start.1 = ((bf16[32,24,1536]{2,1,0:T(8,128)(2,1)}), bf16[32,24,1536]{2,1,0:T(8,128)(2,1)}, u32[]{:S(2)}, u32[]{:S(2)}) async-start(bf16[32,24,1536]{2,1,0:T(8,128)(2,1)} %bitcast.57), calls=%async_computation.1 | async-start | bytes 4718592 | tf_op jit(solution)/shard_map/all_to_all | solution.py:333
  139.8 1.3 convert_add_fusion.1
  141.2 0.8 collective-permute-start.13
  142.0 20.0 %products.1 = (bf16[2,8,192,128]{3,2,1,0:T(8,128)(2,1)}, bf16[2,8,192,128]{3,2,1,0:T(8,128)(2,1)}, bf16[8,384,128]{2,1,0:T(8,128)(2,1)}, bf16[8,384,128]{2,1,0:T(8,128)(2,1)}) custom-call(bf16[2,8,192,128]{3,2,1,0:T(8,128)(2,1)} %bitcast.67, bf16[2,8,192,128]{3,2,1,0:T(8,128)(2,1)} %copy-done.7, bf16[2,8,192,128]{3,2,1,0:T(8,128)(2,1)} %copy-done.6, ...), custom_call_target="tpu_custom_call" | custom-call | flops 14495514624 | bytes 1048576 | tf_op jit(solution)/shard_map/products/pallas_call | solution.py:252
  162.0 14.0 %collective-permute-done.13 = bf16[8,192,128]{2,1,0:T(8,128)(2,1)} collective-permute-done((bf16[8,192,128]{2,1,0:T(8,128)(2,1)S(1)}, bf16[8,192,128]{2,1,0:T(8,128)(2,1)}, u32[]{:S(2)}, u32[]{:S(2)}) %collective-permute-start.13) | collective-permute-done | bytes 393248 | tf_op jit(solution)/shard_map/ppermute | solution.py:285
  176.0 1.1 add_convert_fusion
  177.1 0.5 collective-permute-start.14
  177.6 1.0 convert_reduce_fusion.1
  178.6 1.1 collective-permute-done.14
  179.7 0.2 convert_add_fusion
  180.0 0.9 collective-permute-start.15
  180.9 2.0 %convert_reduce_fusion = f32[24,1536]{1,0:T(8,128)S(1)} fusion(bf16[32,24,1536]{2,1,0:T(8,128)(2,1)} %all-to-all-done.1), kind=kLoop, calls=%fused_computation.1 | loop fusion | flops 2322432 | bytes 2506752 | tf_op jit(solution)/shard_map/reduce_sum | solution.py:336
  182.9 0.8 reshape.57
  183.7 6.7 %collective-permute-done.15 = bf16[8,192,128]{2,1,0:T(8,128)(2,1)S(1)} collective-permute-done((bf16[8,192,128]{2,1,0:T(8,128)(2,1)S(1)}, bf16[8,192,128]{2,1,0:T(8,128)(2,1)S(1)}, u32[]{:S(2)}, u32[]{:S(2)}) %collective-permute-start.15) | collective-permute-done | bytes 393248 | tf_op jit(solution)/shard_map/ppermute | solution.py:285
  190.6 1.0 copy.25
  (49 shorter events, 0.8 us)
Async XLA Ops:
  2.0 6.5 %copy-start = (bf16[1536,4,384]{2,1,0:T(4,128)(2,1)S(1)}, bf16[1536,4,384]{2,1,0:T(4,128)(2,1)}, u32[]{:S(2)}) copy-start(bf16[1536,4,384]{2,1,0:T(4,128)(2,1)} %param.11) | copy-start | bytes 14155780
  5.0 10.4 %copy-start.1 = (bf16[2,8,8,1,24,128]{5,4,3,2,1,0:T(8,128)(2,1)}, bf16[2,8,8,1,24,128]{5,4,3,2,1,0:T(8,128)(2,1)S(1)}, u32[]{:S(2)}) copy-start(bf16[2,8,8,1,24,128]{5,4,3,2,1,0:T(8,128)(2,1)S(1)} %get-tuple-element.85) | copy-start | bytes 2359300
  5.0 21.9 %copy-start.2 = (bf16[2,8,8,1,24,128]{5,4,3,2,1,0:T(8,128)(2,1)}, bf16[2,8,8,1,24,128]{5,4,3,2,1,0:T(8,128)(2,1)S(1)}, u32[]{:S(2)}) copy-start(bf16[2,8,8,1,24,128]{5,4,3,2,1,0:T(8,128)(2,1)S(1)} %get-tuple-element.84) | copy-start | bytes 2359300
  5.0 19.8 %collective-permute-start.1 = (bf16[2,8,192,128]{3,2,1,0:T(8,128)(2,1)S(1)}, bf16[2,8,192,128]{3,2,1,0:T(8,128)(2,1)S(1)}, u32[]{:S(2)}, u32[]{:S(2)}) collective-permute-start(bf16[2,8,192,128]{3,2,1,0:T(8,128)(2,1)S(1)} %bitcast.63), channel_id=1, source_target_pairs={{0,2},{1,3},{2,0},{3,1},{4,6},{5,7},{6,4},{7,5},{8,10},{9,11},{10,... | collective-permute-start | bytes 2359304 | tf_op jit(solution)/shard_map/ppermute | solution.py:285
  7.5 20.8 %collective-permute-start = (bf16[2,8,192,128]{3,2,1,0:T(8,128)(2,1)S(1)}, bf16[2,8,192,128]{3,2,1,0:T(8,128)(2,1)S(1)}, u32[]{:S(2)}, u32[]{:S(2)}) collective-permute-start(bf16[2,8,192,128]{3,2,1,0:T(8,128)(2,1)S(1)} %bitcast.64), channel_id=1, source_target_pairs={{0,1},{1,0},{2,3},{3,2},{4,5},{5,4},{6,7},{7,6},{8,9},{9,8},{10,11... | collective-permute-start | bytes 2359304 | tf_op jit(solution)/shard_map/ppermute | solution.py:285
  24.8 4.5 %copy-start.6 = (bf16[2,8,192,128]{3,2,1,0:T(8,128)(2,1)}, bf16[2,8,192,128]{3,2,1,0:T(8,128)(2,1)S(1)}, u32[]{:S(2)}) copy-start(bf16[2,8,192,128]{3,2,1,0:T(8,128)(2,1)S(1)} %collective-permute-done.1.refs_2_) | copy-start | bytes 2359300
  24.8 3.5 %collective-permute-start.2 = (bf16[2,8,192,128]{3,2,1,0:T(8,128)(2,1)S(1)}, bf16[2,8,192,128]{3,2,1,0:T(8,128)(2,1)}, u32[]{:S(2)}, u32[]{:S(2)}) collective-permute-start(bf16[2,8,192,128]{3,2,1,0:T(8,128)(2,1)S(1)} %collective-permute-done.1.refs_2_), channel_id=1, source_target_pairs={{0,1},{1,0},{2,3},{3,2},{4,5},{5,4},{6,7},{7,6},{8,9},{9,8},{10,11... | collective-permute-start | bytes 2359304 | tf_op jit(solution)/shard_map/ppermute | solution.py:285
  26.8 22.3 %collective-permute-start.7 = (bf16[2,8,192,128]{3,2,1,0:T(8,128)(2,1)S(1)}, bf16[2,8,192,128]{3,2,1,0:T(8,128)(2,1)}, u32[]{:S(2)}, u32[]{:S(2)}) collective-permute-start(bf16[2,8,192,128]{3,2,1,0:T(8,128)(2,1)S(1)} %bitcast.68), channel_id=1, source_target_pairs={{0,1},{1,0},{2,3},{3,2},{4,5},{5,4},{6,7},{7,6},{8,9},{9,8},{10,11... | collective-permute-start | bytes 2359304 | tf_op jit(solution)/shard_map/ppermute | solution.py:285
  26.8 18.8 %collective-permute-start.3 = (bf16[2,8,192,128]{3,2,1,0:T(8,128)(2,1)S(1)}, bf16[2,8,192,128]{3,2,1,0:T(8,128)(2,1)}, u32[]{:S(2)}, u32[]{:S(2)}) collective-permute-start(bf16[2,8,192,128]{3,2,1,0:T(8,128)(2,1)S(1)} %bitcast.69), channel_id=1, source_target_pairs={{0,2},{1,3},{2,0},{3,1},{4,6},{5,7},{6,4},{7,5},{8,10},{9,11},{10,... | collective-permute-start | bytes 2359304 | tf_op jit(solution)/shard_map/ppermute | solution.py:285
  28.3 1.0 copy-start.7
  45.6 3.5 %collective-permute-start.8 = (bf16[2,8,192,128]{3,2,1,0:T(8,128)(2,1)}, bf16[2,8,192,128]{3,2,1,0:T(8,128)(2,1)S(1)}, u32[]{:S(2)}, u32[]{:S(2)}) collective-permute-start(bf16[2,8,192,128]{3,2,1,0:T(8,128)(2,1)} %collective-permute-done.3.refs_2_), channel_id=1, source_target_pairs={{0,1},{1,0},{2,3},{3,2},{4,5},{5,4},{6,7},{7,6},{8,9},{9,8},{10,11... | collective-permute-start | bytes 2359304 | tf_op jit(solution)/shard_map/ppermute | solution.py:285
  46.9 17.6 %collective-permute-start.6 = (f32[4,8,8,192]{3,2,1,0:T(8,128)}, f32[4,8,8,192]{3,2,1,0:T(8,128)S(1)}, u32[]{:S(2)}, u32[]{:S(2)}) collective-permute-start(f32[4,8,8,192]{3,2,1,0:T(8,128)} %totals.2.refs_11_), channel_id=1, source_target_pairs={{0,3},{1,2},{2,1},{3,0},{4,7},{5,6},{6,5},{7,4},{8,11},{9,10},{10,... | collective-permute-start | bytes 589832 | tf_op jit(solution)/shard_map/ppermute | solution.py:285
  48.3 16.3 %collective-permute-start.5 = (f32[4,8,8,192]{3,2,1,0:T(8,128)}, f32[4,8,8,192]{3,2,1,0:T(8,128)S(1)}, u32[]{:S(2)}, u32[]{:S(2)}) collective-permute-start(f32[4,8,8,192]{3,2,1,0:T(8,128)} %totals.2.refs_11_), channel_id=1, source_target_pairs={{0,2},{1,3},{2,0},{3,1},{4,6},{5,7},{6,4},{7,5},{8,10},{9,11},{10,... | collective-permute-start | bytes 589832 | tf_op jit(solution)/shard_map/ppermute | solution.py:285
  48.4 16.2 %collective-permute-start.4 = (f32[4,8,8,192]{3,2,1,0:T(8,128)}, f32[4,8,8,192]{3,2,1,0:T(8,128)S(1)}, u32[]{:S(2)}, u32[]{:S(2)}) collective-permute-start(f32[4,8,8,192]{3,2,1,0:T(8,128)} %totals.2.refs_11_), channel_id=1, source_target_pairs={{0,1},{1,0},{2,3},{3,2},{4,5},{5,4},{6,7},{7,6},{8,9},{9,8},{10,11... | collective-permute-start | bytes 589832 | tf_op jit(solution)/shard_map/ppermute | solution.py:285
  49.1 0.9 copy-start.8
  64.5 2.9 %copy-start.10 = (f32[4,8,8,192]{3,2,1,0:T(8,128)}, f32[4,8,8,192]{3,2,1,0:T(8,128)S(1)}, u32[]{:S(2)}) copy-start(f32[4,8,8,192]{3,2,1,0:T(8,128)S(1)} %collective-permute-done.6.refs_14_) | copy-start | bytes 589828
  64.6 2.9 %copy-start.12 = (f32[4,8,8,192]{3,2,1,0:T(8,128)}, f32[4,8,8,192]{3,2,1,0:T(8,128)S(1)}, u32[]{:S(2)}) copy-start(f32[4,8,8,192]{3,2,1,0:T(8,128)S(1)} %collective-permute-done.5.refs_13_) | copy-start | bytes 589828
  64.6 2.9 %copy-start.14 = (f32[4,8,8,192]{3,2,1,0:T(8,128)}, f32[4,8,8,192]{3,2,1,0:T(8,128)S(1)}, u32[]{:S(2)}) copy-start(f32[4,8,8,192]{3,2,1,0:T(8,128)S(1)} %collective-permute-done.4.refs_12_) | copy-start | bytes 589828
  64.6 24.2 %collective-permute-start.11 = (f32[4,8,8,192]{3,2,1,0:T(8,128)}, f32[4,8,8,192]{3,2,1,0:T(8,128)S(1)}, u32[]{:S(2)}, u32[]{:S(2)}) collective-permute-start(f32[4,8,8,192]{3,2,1,0:T(8,128)} %totals.3.refs_11_), channel_id=1, source_target_pairs={{0,3},{1,2},{2,1},{3,0},{4,7},{5,6},{6,5},{7,4},{8,11},{9,10},{10,... | collective-permute-start | bytes 589832 | tf_op jit(solution)/shard_map/ppermute | solution.py:285
  66.3 22.5 %collective-permute-start.10 = (f32[4,8,8,192]{3,2,1,0:T(8,128)}, f32[4,8,8,192]{3,2,1,0:T(8,128)S(1)}, u32[]{:S(2)}, u32[]{:S(2)}) collective-permute-start(f32[4,8,8,192]{3,2,1,0:T(8,128)} %totals.3.refs_11_), channel_id=1, source_target_pairs={{0,2},{1,3},{2,0},{3,1},{4,6},{5,7},{6,4},{7,5},{8,10},{9,11},{10,... | collective-permute-start | bytes 589832 | tf_op jit(solution)/shard_map/ppermute | solution.py:285
  66.4 22.5 %collective-permute-start.9 = (f32[4,8,8,192]{3,2,1,0:T(8,128)}, f32[4,8,8,192]{3,2,1,0:T(8,128)S(1)}, u32[]{:S(2)}, u32[]{:S(2)}) collective-permute-start(f32[4,8,8,192]{3,2,1,0:T(8,128)} %totals.3.refs_11_), channel_id=1, source_target_pairs={{0,1},{1,0},{2,3},{3,2},{4,5},{5,4},{6,7},{7,6},{8,9},{9,8},{10,11... | collective-permute-start | bytes 589832 | tf_op jit(solution)/shard_map/ppermute | solution.py:285
  88.8 0.7 copy-start.9
  88.8 0.8 copy-start.11
  88.9 0.8 copy-start.13
  89.7 42.7 %all-to-all-start = ((bf16[32,24,1536]{2,1,0:T(8,128)(2,1)}), bf16[32,24,1536]{2,1,0:T(8,128)(2,1)S(1)}, u32[]{:S(2)}, u32[]{:S(2)}) async-start(bf16[32,24,1536]{2,1,0:T(8,128)(2,1)} %bitcast.58), calls=%async_computation | async-start | bytes 4718592 | tf_op jit(solution)/shard_map/all_to_all | solution.py:333
  132.4 7.3 %collective-permute-start.12 = (bf16[2,8,192,128]{3,2,1,0:T(8,128)(2,1)}, bf16[2,8,192,128]{3,2,1,0:T(8,128)(2,1)}, u32[]{:S(2)}, u32[]{:S(2)}) collective-permute-start(bf16[2,8,192,128]{3,2,1,0:T(8,128)(2,1)} %get-tuple-element.63), channel_id=1, source_target_pairs={{0,1},{1,0},{2,3},{3,2},{4,5},{5,4},{6,7},{7,6},{8,9},{9,8},{10,11... | collective-permute-start | bytes 2359304 | tf_op jit(solution)/shard_map/ppermute | solution.py:285
  133.4 6.3 %copy-start.3 = (bf16[2,8,192,128]{3,2,1,0:T(8,128)(2,1)S(1)}, bf16[2,8,192,128]{3,2,1,0:T(8,128)(2,1)}, u32[]{:S(2)}) copy-start(bf16[2,8,192,128]{3,2,1,0:T(8,128)(2,1)} %get-tuple-element.62) | copy-start | bytes 2359300
  133.4 47.4 %all-to-all-start.1 = ((bf16[32,24,1536]{2,1,0:T(8,128)(2,1)}), bf16[32,24,1536]{2,1,0:T(8,128)(2,1)}, u32[]{:S(2)}, u32[]{:S(2)}) async-start(bf16[32,24,1536]{2,1,0:T(8,128)(2,1)} %bitcast.57), calls=%async_computation.1 | async-start | bytes 4718592 | tf_op jit(solution)/shard_map/all_to_all | solution.py:333
  141.2 34.8 %collective-permute-start.13 = (bf16[8,192,128]{2,1,0:T(8,128)(2,1)S(1)}, bf16[8,192,128]{2,1,0:T(8,128)(2,1)}, u32[]{:S(2)}, u32[]{:S(2)}) collective-permute-start(bf16[8,192,128]{2,1,0:T(8,128)(2,1)S(1)} %fusion.3), channel_id=1, source_target_pairs={{0,2},{1,3},{2,0},{3,1},{4,6},{5,7},{6,4},{7,5},{8,10},{9,11},{10,... | collective-permute-start | bytes 1179656 | tf_op jit(solution)/shard_map/ppermute | solution.py:285
  162.0 17.7 %copy-start.4 = (bf16[2,8,192,128]{3,2,1,0:T(8,128)(2,1)S(1)}, bf16[2,8,192,128]{3,2,1,0:T(8,128)(2,1)}, u32[]{:S(2)}) copy-start(bf16[2,8,192,128]{3,2,1,0:T(8,128)(2,1)} %get-tuple-element.73) | copy-start | bytes 2359300
  177.1 2.7 %collective-permute-start.14 = (bf16[2,8,192,128]{3,2,1,0:T(8,128)(2,1)}, bf16[2,8,192,128]{3,2,1,0:T(8,128)(2,1)S(1)}, u32[]{:S(2)}, u32[]{:S(2)}) collective-permute-start(bf16[2,8,192,128]{3,2,1,0:T(8,128)(2,1)} %get-tuple-element.74), channel_id=1, source_target_pairs={{0,1},{1,0},{2,3},{3,2},{4,5},{5,4},{6,7},{7,6},{8,9},{9,8},{10,11... | collective-permute-start | bytes 2359304 | tf_op jit(solution)/shard_map/ppermute | solution.py:285
  179.9 3.0 %copy-start.5 = (f32[24,1536]{1,0:T(8,128)S(1)}, f32[24,1536]{1,0:T(8,128)}, u32[]{:S(2)}) copy-start(f32[24,1536]{1,0:T(8,128)} %convert_reduce_fusion.1) | copy-start | bytes 442372
  180.0 10.4 %collective-permute-start.15 = (bf16[8,192,128]{2,1,0:T(8,128)(2,1)S(1)}, bf16[8,192,128]{2,1,0:T(8,128)(2,1)S(1)}, u32[]{:S(2)}, u32[]{:S(2)}) collective-permute-start(bf16[8,192,128]{2,1,0:T(8,128)(2,1)S(1)} %fusion.4), channel_id=1, source_target_pairs={{0,2},{1,3},{2,0},{3,1},{4,6},{5,7},{6,4},{7,5},{8,10},{9,11},{10,... | collective-permute-start | bytes 1179656 | tf_op jit(solution)/shard_map/ppermute | solution.py:285

commit v2 on v1

--- a/solution.py
+++ b/solution.py
@@ -197,7 +197,7 @@
     parts, biases, refs = refs[:4], refs[4:8], refs[8:]
     k_ref, v_ref, gate_ref, *refs = refs
     stats, refs = refs[:4], refs[4:]
-    p_ref, ds_ref, db_ref, kx_ref, vx_ref, sum_ref, bias_ref = refs
+    dv_ref, ds_ref, db_ref, kx_ref, vx_ref, sum_ref, bias_ref, p_ref = refs
     col = col_ref[0]
     prepare(biases, gate_ref, sum_ref, bias_ref, kx_ref, vx_ref, k_ref[0], v_ref[0])
     qx, gx = with_extra(joined(parts, 0), joined(parts, 1), stats, col)
@@ -205,23 +205,27 @@
         at = slice(n * TILE, (n + 1) * TILE)
         p, ds = chances(qx, gx, kx_ref, vx_ref, bias_ref, at)
         sum_ref[:, at] += ds
-        p_ref[0, :, at] = p.astype(BF16)
+        p_ref[:, at] = p.astype(BF16)
         ds_ref[0, :, at] = ds.astype(BF16)
+    gt, key_len = joined(parts, 1).T, k_ref.shape[1]
+    for h in range(HEADS):
+        rows, at = slice(h * HEAD_DIM, (h + 1) * HEAD_DIM), slice(h * key_len, (h + 1) * key_len)
+        dv_ref[0, rows] = jnp.dot(gt[rows], p_ref[:, at], preferred_element_type=F32)
     store_bias(col, sum_ref, db_ref)
 
 
 def products_kernel(*refs):
     parts, refs = refs[:4], refs[4:]
-    k_ref, p_ref, ds_ref, dk_in, dv_in, *refs = refs
+    k_ref, dv_first, ds_ref, dk_in, dv_in, *refs = refs
     dq_refs, (dk_out, dv_out, kx_ref, dk_ref, dv_ref) = refs[:2], refs[2:]
     q, g = joined(parts, 0), joined(parts, 1)
     key_len = k_ref.shape[1]
     load_keys(kx_ref, k_ref[0])
     store_queries(jnp.dot(ds_ref[0], kx_ref[...], preferred_element_type=F32), dq_refs)
-    qt, gt = q.T, g.T
+    qt = q.T
     for h in range(HEADS):
         rows, at = slice(h * HEAD_DIM, (h + 1) * HEAD_DIM), slice(h * key_len, (h + 1) * key_len)
-        dv_ref[rows] = jnp.dot(gt[rows], p_ref[0, :, at], preferred_element_type=F32) + dv_in[0, rows]
+        dv_ref[rows] = dv_first[0, rows] + dv_in[0, rows]
         dk = jnp.dot(qt[rows], ds_ref[0, :, at], preferred_element_type=F32)
         dk_ref[rows] = (dk + dk_in[0, rows]) * SCALE
     dv_out[0] = dv_ref[...].T.astype(BF16)
@@ -253,7 +257,7 @@
             products_kernel,
             grid=(rows,),
             in_specs=[pl.BlockSpec((2, 1, part_len, CH), lambda i: (0, i, 0, 0))] * 4
-            + [data, square, square, side, side],
+            + [data, side, square, side, side],
             out_specs=dq_specs + [data, data],
             out_shape=dq_shapes + [data_shape, data_shape],
             scratch_shapes=[pltpu.VMEM((width, CH), BF16), pltpu.VMEM((CH, key_len), F32), pltpu.VMEM((CH, key_len), F32)],
@@ -263,8 +267,8 @@
         )(*parts, keys, *carried)
     in_specs = part_specs(part_len, bias, chunk) + [data, data, pl.BlockSpec((8, key_len), whole)] + stat_specs
     if kind == "chances":
-        out_specs, out_shape = [square, square, db_spec], [square_shape, square_shape, db_shape]
-        scratch = [keys_scratch, keys_scratch, wide, wide]
+        out_specs, out_shape = [side, square, db_spec], [side_shape, square_shape, db_shape]
+        scratch = [keys_scratch, keys_scratch, wide, wide, low]
     else:
         out_specs = dq_specs + [side, side, db_spec]
         out_shape = dq_shapes + [side_shape, side_shape, db_shape]

time: 192 us -> 192 us (level)
  waiting for transfers between devices: 32.5 us -> 36.6 us
  Pallas kernels: 99.7 us -> 96 us
    pallas_call x1, Pallas kernels: 20 us -> 15.8 us  [grads(): pl.pallas_call(products_kernel, grid=(rows,), in_specs=[pl.BlockSpec((2,...]
    ppermute x16, waiting for transfers between devices: 29.1 us -> 33.3 us  [partner(): return lax.ppermute(x, 'cols', [(c, c ^ distance) for c in range(4)])]
  transfers between devices with their start and end apart: 18 -> 18, of which waited for: 6 -> 6; matrix products, arithmetic and copies ran while one was open for 10% -> 10% of each run, Pallas kernels for 52% -> 50%
where the time goes in v2:
time: 192 us
  Pallas kernels  96 us (50%)
  waiting for transfers between devices  36.6 us (19%)
  starting transfers between devices  31.5 us (16%)
  local copies, waits for them, and re-layouts  15.4 us (8%)
  other arithmetic  10.8 us (6%)
    pallas_call x2, Pallas kernels, grads(): pl.pallas_call(chances_kernel if kind == 'chances' else grads_kernel, gri...  51 us
    ppermute x16, waiting for transfers between devices, partner(): return lax.ppermute(x, 'cols', [(c, c ^ distance) for c in range(4)])  33.3 us
    pallas_call x2, Pallas kernels, totals(): pl.pallas_call(totals_kernel, grid_spec=pltpu.PrefetchScalarGridSpec(num_...  29.2 us
    all_to_all x2, starting transfers between devices, swap_bias(): return lax.all_to_all(db.reshape(32, step, width), 'rows', 0, 0, tiled=True)  16.3 us
    pallas_call x1, Pallas kernels, grads(): pl.pallas_call(products_kernel, grid=(rows,), in_specs=[pl.BlockSpec((2,...  15.8 us
    ppermute x16, starting transfers between devices, partner(): return lax.ppermute(x, 'cols', [(c, c ^ distance) for c in range(4)])  15.1 us
    slice x1, local copies, waits for them, and re-layouts, per_device(): bias = jnp.concatenate([pair_bias[:, h] for h in range(HEADS)], axis=1)  6.84 us
  transfers between devices with their start and end apart: 18, of which 6 were waited for; matrix products, arithmetic and copies ran while one was open for 10% of the time, Pallas kernels for 50%

profile of v2, /device:TPU:1, one launch (start us, length us, event | category | flops | bytes accessed | tf_op | source)
XLA Modules:
  0.0 191.9 jit_solution(12671876733305839202)
XLA Ops:
  1.3 0.8 dynamic-slice_convert_fusion
  2.0 1.4 broadcast_multiply_fusion
  3.5 1.5 pad_maximum_fusion
  5.0 2.5 %collective-permute-start.1 = (bf16[2,8,192,128]{3,2,1,0:T(8,128)(2,1)S(1)}, bf16[2,8,192,128]{3,2,1,0:T(8,128)(2,1)S(1)}, u32[]{:S(2)}, u32[]{:S(2)}) collective-permute-start(bf16[2,8,192,128]{3,2,1,0:T(8,128)(2,1)S(1)} %bitcast.63), channel_id=1, source_target_pairs={{0,2},{1,3},{2,0},{3,1},{4,6},{5,7},{6,4},{7,5},{8,10},{9,11},{10,... | collective-permute-start | bytes 2359304 | tf_op jit(solution)/shard_map/ppermute | solution.py:289
  7.5 1.0 collective-permute-start
  8.5 6.8 %fusion.6 = (bf16[1536,1,384]{2,1,0:T(2,128)(2,1)S(1)}, bf16[1536,1,384]{2,1,0:T(2,128)(2,1)S(1)}, bf16[1536,1,384]{2,1,0:T(2,128)(2,1)S(1)}, bf16[1536,1,384]{2,1,0:T(2,128)(2,1)S(1)}) fusion(bf16[1536,4,384]{2,1,0:T(4,128)(2,1)S(1)} %copy-done), kind=kLoop, calls=%fused_computation.24 | loop fusion | bytes 9437184 | tf_op jit(solution)/shard_map/slice | solution.py:310
  15.4 0.2 copy.28
  15.6 0.2 copy.30
  15.8 0.2 copy.29
  16.0 0.2 copy.31
  16.2 0.6 maximum_bitcast_fusion
  16.8 2.5 %copy.24 = bf16[2,32,24,1536]{3,2,1,0:T(8,128)(2,1)} copy(bf16[2,32,24,1536]{3,2,0,1:T(8,128)(2,1)S(1)} %maximum_bitcast_fusion) | data formatting | bytes 9437184 | tf_op jit(solution)/shard_map/transpose | solution.py:311
  19.3 5.5 %collective-permute-done.1.refs_2_ = bf16[2,8,192,128]{3,2,1,0:T(8,128)(2,1)S(1)} collective-permute-done((bf16[2,8,192,128]{3,2,1,0:T(8,128)(2,1)S(1)}, bf16[2,8,192,128]{3,2,1,0:T(8,128)(2,1)S(1)}, u32[]{:S(2)}, u32[]{:S(2)}) %collective-permute-start.1) | collective-permute-done | bytes 786464 | tf_op jit(solution)/shard_map/ppermute | solution.py:289
  24.8 1.3 collective-permute-start.2
  26.0 0.8 fusion.5
  26.8 1.5 collective-permute-start.3
  28.3 0.9 broadcast_in_dim.24.refs_10_
  29.3 14.6 %totals.2.refs_11_ = f32[4,8,8,192]{3,2,1,0:T(8,128)} custom-call(s32[1]{0:T(128)} %bitcast.col_ref, bf16[2,8,192,128]{3,2,1,0:T(8,128)(2,1)} %bitcast.65, bf16[2,8,192,128]{3,2,1,0:T(8,128)(2,1)} %copy-done.7, bf16[2,8,192,128]{3,2,1,0:T(8,128)(2,1)} %copy-done.6, bf16[2,8,192,128]{3,2,1,0:T(8,128)(2,1)} %collective-permute-done.2.refs_3_, ...), custom_call_target="tpu_custom_call" | custom-call | flops 14495514624 | bytes 1048576 | tf_op jit(solution)/shard_map/totals/pallas_call | solution.py:83
  43.9 1.7 collective-permute-done.3.refs_2_
  45.6 1.3 collective-permute-start.8
  46.9 1.3 collective-permute-start.6
  48.4 0.7 collective-permute-start.4
  49.1 0.9 copy-done.8
  50.0 14.6 %totals.3.refs_11_ = f32[4,8,8,192]{3,2,1,0:T(8,128)} custom-call(s32[1]{0:T(128)} %bitcast.col_ref, bf16[2,8,192,128]{3,2,1,0:T(8,128)(2,1)} %bitcast.70, bf16[2,8,192,128]{3,2,1,0:T(8,128)(2,1)} %collective-permute-done.7.refs_1_, bf16[2,8,192,128]{3,2,1,0:T(8,128)(2,1)} %collective-permute-done.3.refs_2_, bf16[2,8,192,128]{3,2,1,0:T(8,128)(2,1)} %copy-done.8, ...), custom_call_target="tpu_custom_call" | custom-call | flops 14495514624 | bytes 1048576 | tf_op jit(solution)/shard_map/totals/pallas_call | solution.py:83
  64.6 1.8 collective-permute-start.11
  66.4 0.5 collective-permute-start.9
  66.8 0.6 broadcast_in_dim.23.refs_10_
  67.4 21.8 %chances.1 = (f32[8,128,384]{2,1,0:T(8,128)}, bf16[8,768,1536]{2,1,0:T(8,128)(2,1)}, bf16[4,192,1536]{2,1,0:T(8,128)(2,1)}) custom-call(s32[1]{0:T(128)} %bitcast.col_ref, bf16[2,8,192,128]{3,2,1,0:T(8,128)(2,1)} %bitcast.66, bf16[2,8,192,128]{3,2,1,0:T(8,128)(2,1)} %copy-done.7, bf16[2,8,192,128]{3,2,1,0:T(8,128)(2,1)} %copy-done.6, ...), custom_call_target="tpu_custom_call" | custom-call | flops 19327352832 | bytes 1048576 | tf_op jit(solution)/shard_map/chances/pallas_call | solution.py:276
  89.3 0.7 copy-done.9
  90.2 10.1 %all-to-all-start = ((bf16[32,24,1536]{2,1,0:T(8,128)(2,1)}), bf16[32,24,1536]{2,1,0:T(8,128)(2,1)S(1)}, u32[]{:S(2)}, u32[]{:S(2)}) async-start(bf16[32,24,1536]{2,1,0:T(8,128)(2,1)} %bitcast.58), calls=%async_computation | async-start | bytes 4718592 | tf_op jit(solution)/shard_map/all_to_all | solution.py:337
  100.3 29.2 %grads.1 = (bf16[2,8,192,128]{3,2,1,0:T(8,128)(2,1)}, bf16[2,8,192,128]{3,2,1,0:T(8,128)(2,1)}, f32[8,128,384]{2,1,0:T(8,128)}, f32[8,128,384]{2,1,0:T(8,128)}, bf16[4,192,1536]{2,1,0:T(8,128)(2,1)}) custom-call(s32[1]{0:T(128)} %bitcast.col_ref, bf16[2,8,192,128]{3,2,1,0:T(8,128)(2,1)} %bitcast.71, bf16[2,8,192,128]{3,2,1,0:T(8,128)(2,1)} %collective-permute-done.7.refs_1_, ...), custom_call_target="tpu_custom_call" | custom-call | flops 28991029248 | bytes 1048576 | tf_op jit(solution)/shard_map/grads/pallas_call | solution.py:276
  129.5 3.3 %all-to-all-done = bf16[32,24,1536]{2,1,0:T(8,128)(2,1)S(1)} async-done(((bf16[32,24,1536]{2,1,0:T(8,128)(2,1)}), bf16[32,24,1536]{2,1,0:T(8,128)(2,1)S(1)}, u32[]{:S(2)}, u32[]{:S(2)}) %all-to-all-start) | async-done | bytes 2359328 | tf_op jit(solution)/shard_map/all_to_all | solution.py:337
  132.8 1.0 collective-permute-start.12
  133.8 6.2 %all-to-all-start.1 = ((bf16[32,24,1536]{2,1,0:T(8,128)(2,1)}), bf16[32,24,1536]{2,1,0:T(8,128)(2,1)}, u32[]{:S(2)}, u32[]{:S(2)}) async-start(bf16[32,24,1536]{2,1,0:T(8,128)(2,1)} %bitcast.57), calls=%async_computation.1 | async-start | bytes 4718592 | tf_op jit(solution)/shard_map/all_to_all | solution.py:337
  140.1 1.3 convert_add_fusion.1
  141.5 0.8 collective-permute-start.13
  142.3 15.8 %products.1 = (bf16[2,8,192,128]{3,2,1,0:T(8,128)(2,1)}, bf16[2,8,192,128]{3,2,1,0:T(8,128)(2,1)}, bf16[8,384,128]{2,1,0:T(8,128)(2,1)}, bf16[8,384,128]{2,1,0:T(8,128)(2,1)}) custom-call(bf16[2,8,192,128]{3,2,1,0:T(8,128)(2,1)} %bitcast.67, bf16[2,8,192,128]{3,2,1,0:T(8,128)(2,1)} %copy-done.7, bf16[2,8,192,128]{3,2,1,0:T(8,128)(2,1)} %copy-done.6, ...), custom_call_target="tpu_custom_call" | custom-call | flops 14495514624 | bytes 1048576 | tf_op jit(solution)/shard_map/products/pallas_call | solution.py:256
  158.1 18.2 %collective-permute-done.13 = bf16[8,192,128]{2,1,0:T(8,128)(2,1)} collective-permute-done((bf16[8,192,128]{2,1,0:T(8,128)(2,1)S(1)}, bf16[8,192,128]{2,1,0:T(8,128)(2,1)}, u32[]{:S(2)}, u32[]{:S(2)}) %collective-permute-start.13) | collective-permute-done | bytes 393248 | tf_op jit(solution)/shard_map/ppermute | solution.py:289
  176.3 1.1 add_convert_fusion
  177.4 0.5 collective-permute-start.14
  177.9 1.0 convert_reduce_fusion.1
  178.9 1.1 collective-permute-done.14
  180.0 0.2 convert_add_fusion
  180.3 0.8 collective-permute-start.15
  181.2 2.0 %convert_reduce_fusion = f32[24,1536]{1,0:T(8,128)S(1)} fusion(bf16[32,24,1536]{2,1,0:T(8,128)(2,1)} %all-to-all-done.1), kind=kLoop, calls=%fused_computation.1 | loop fusion | flops 2322432 | bytes 2506752 | tf_op jit(solution)/shard_map/reduce_sum | solution.py:340
  183.2 0.8 reshape.57
  184.0 6.7 %collective-permute-done.15 = bf16[8,192,128]{2,1,0:T(8,128)(2,1)S(1)} collective-permute-done((bf16[8,192,128]{2,1,0:T(8,128)(2,1)S(1)}, bf16[8,192,128]{2,1,0:T(8,128)(2,1)S(1)}, u32[]{:S(2)}, u32[]{:S(2)}) %collective-permute-start.15) | collective-permute-done | bytes 393248 | tf_op jit(solution)/shard_map/ppermute | solution.py:289
  190.9 1.0 copy.25
  (49 shorter events, 0.8 us)
Async XLA Ops:
  2.0 6.5 %copy-start = (bf16[1536,4,384]{2,1,0:T(4,128)(2,1)S(1)}, bf16[1536,4,384]{2,1,0:T(4,128)(2,1)}, u32[]{:S(2)}) copy-start(bf16[1536,4,384]{2,1,0:T(4,128)(2,1)} %param.11) | copy-start | bytes 14155780
  5.0 10.4 %copy-start.1 = (bf16[2,8,8,1,24,128]{5,4,3,2,1,0:T(8,128)(2,1)}, bf16[2,8,8,1,24,128]{5,4,3,2,1,0:T(8,128)(2,1)S(1)}, u32[]{:S(2)}) copy-start(bf16[2,8,8,1,24,128]{5,4,3,2,1,0:T(8,128)(2,1)S(1)} %get-tuple-element.85) | copy-start | bytes 2359300
  5.0 21.9 %copy-start.2 = (bf16[2,8,8,1,24,128]{5,4,3,2,1,0:T(8,128)(2,1)}, bf16[2,8,8,1,24,128]{5,4,3,2,1,0:T(8,128)(2,1)S(1)}, u32[]{:S(2)}) copy-start(bf16[2,8,8,1,24,128]{5,4,3,2,1,0:T(8,128)(2,1)S(1)} %get-tuple-element.84) | copy-start | bytes 2359300
  5.0 19.8 %collective-permute-start.1 = (bf16[2,8,192,128]{3,2,1,0:T(8,128)(2,1)S(1)}, bf16[2,8,192,128]{3,2,1,0:T(8,128)(2,1)S(1)}, u32[]{:S(2)}, u32[]{:S(2)}) collective-permute-start(bf16[2,8,192,128]{3,2,1,0:T(8,128)(2,1)S(1)} %bitcast.63), channel_id=1, source_target_pairs={{0,2},{1,3},{2,0},{3,1},{4,6},{5,7},{6,4},{7,5},{8,10},{9,11},{10,... | collective-permute-start | bytes 2359304 | tf_op jit(solution)/shard_map/ppermute | solution.py:289
  7.5 20.8 %collective-permute-start = (bf16[2,8,192,128]{3,2,1,0:T(8,128)(2,1)S(1)}, bf16[2,8,192,128]{3,2,1,0:T(8,128)(2,1)S(1)}, u32[]{:S(2)}, u32[]{:S(2)}) collective-permute-start(bf16[2,8,192,128]{3,2,1,0:T(8,128)(2,1)S(1)} %bitcast.64), channel_id=1, source_target_pairs={{0,1},{1,0},{2,3},{3,2},{4,5},{5,4},{6,7},{7,6},{8,9},{9,8},{10,11... | collective-permute-start | bytes 2359304 | tf_op jit(solution)/shard_map/ppermute | solution.py:289
  24.8 4.5 %copy-start.6 = (bf16[2,8,192,128]{3,2,1,0:T(8,128)(2,1)}, bf16[2,8,192,128]{3,2,1,0:T(8,128)(2,1)S(1)}, u32[]{:S(2)}) copy-start(bf16[2,8,192,128]{3,2,1,0:T(8,128)(2,1)S(1)} %collective-permute-done.1.refs_2_) | copy-start | bytes 2359300
  24.8 3.5 %collective-permute-start.2 = (bf16[2,8,192,128]{3,2,1,0:T(8,128)(2,1)S(1)}, bf16[2,8,192,128]{3,2,1,0:T(8,128)(2,1)}, u32[]{:S(2)}, u32[]{:S(2)}) collective-permute-start(bf16[2,8,192,128]{3,2,1,0:T(8,128)(2,1)S(1)} %collective-permute-done.1.refs_2_), channel_id=1, source_target_pairs={{0,1},{1,0},{2,3},{3,2},{4,5},{5,4},{6,7},{7,6},{8,9},{9,8},{10,11... | collective-permute-start | bytes 2359304 | tf_op jit(solution)/shard_map/ppermute | solution.py:289
  26.8 22.3 %collective-permute-start.7 = (bf16[2,8,192,128]{3,2,1,0:T(8,128)(2,1)S(1)}, bf16[2,8,192,128]{3,2,1,0:T(8,128)(2,1)}, u32[]{:S(2)}, u32[]{:S(2)}) collective-permute-start(bf16[2,8,192,128]{3,2,1,0:T(8,128)(2,1)S(1)} %bitcast.68), channel_id=1, source_target_pairs={{0,1},{1,0},{2,3},{3,2},{4,5},{5,4},{6,7},{7,6},{8,9},{9,8},{10,11... | collective-permute-start | bytes 2359304 | tf_op jit(solution)/shard_map/ppermute | solution.py:289
  26.8 18.8 %collective-permute-start.3 = (bf16[2,8,192,128]{3,2,1,0:T(8,128)(2,1)S(1)}, bf16[2,8,192,128]{3,2,1,0:T(8,128)(2,1)}, u32[]{:S(2)}, u32[]{:S(2)}) collective-permute-start(bf16[2,8,192,128]{3,2,1,0:T(8,128)(2,1)S(1)} %bitcast.69), channel_id=1, source_target_pairs={{0,2},{1,3},{2,0},{3,1},{4,6},{5,7},{6,4},{7,5},{8,10},{9,11},{10,... | collective-permute-start | bytes 2359304 | tf_op jit(solution)/shard_map/ppermute | solution.py:289
  28.3 1.0 copy-start.7
  45.6 3.5 %collective-permute-start.8 = (bf16[2,8,192,128]{3,2,1,0:T(8,128)(2,1)}, bf16[2,8,192,128]{3,2,1,0:T(8,128)(2,1)S(1)}, u32[]{:S(2)}, u32[]{:S(2)}) collective-permute-start(bf16[2,8,192,128]{3,2,1,0:T(8,128)(2,1)} %collective-permute-done.3.refs_2_), channel_id=1, source_target_pairs={{0,1},{1,0},{2,3},{3,2},{4,5},{5,4},{6,7},{7,6},{8,9},{9,8},{10,11... | collective-permute-start | bytes 2359304 | tf_op jit(solution)/shard_map/ppermute | solution.py:289
  46.9 17.6 %collective-permute-start.6 = (f32[4,8,8,192]{3,2,1,0:T(8,128)}, f32[4,8,8,192]{3,2,1,0:T(8,128)S(1)}, u32[]{:S(2)}, u32[]{:S(2)}) collective-permute-start(f32[4,8,8,192]{3,2,1,0:T(8,128)} %totals.2.refs_11_), channel_id=1, source_target_pairs={{0,3},{1,2},{2,1},{3,0},{4,7},{5,6},{6,5},{7,4},{8,11},{9,10},{10,... | collective-permute-start | bytes 589832 | tf_op jit(solution)/shard_map/ppermute | solution.py:289
  48.3 16.3 %collective-permute-start.5 = (f32[4,8,8,192]{3,2,1,0:T(8,128)}, f32[4,8,8,192]{3,2,1,0:T(8,128)S(1)}, u32[]{:S(2)}, u32[]{:S(2)}) collective-permute-start(f32[4,8,8,192]{3,2,1,0:T(8,128)} %totals.2.refs_11_), channel_id=1, source_target_pairs={{0,2},{1,3},{2,0},{3,1},{4,6},{5,7},{6,4},{7,5},{8,10},{9,11},{10,... | collective-permute-start | bytes 589832 | tf_op jit(solution)/shard_map/ppermute | solution.py:289
  48.4 16.2 %collective-permute-start.4 = (f32[4,8,8,192]{3,2,1,0:T(8,128)}, f32[4,8,8,192]{3,2,1,0:T(8,128)S(1)}, u32[]{:S(2)}, u32[]{:S(2)}) collective-permute-start(f32[4,8,8,192]{3,2,1,0:T(8,128)} %totals.2.refs_11_), channel_id=1, source_target_pairs={{0,1},{1,0},{2,3},{3,2},{4,5},{5,4},{6,7},{7,6},{8,9},{9,8},{10,11... | collective-permute-start | bytes 589832 | tf_op jit(solution)/shard_map/ppermute | solution.py:289
  49.1 0.9 copy-start.8
  64.5 2.9 %copy-start.10 = (f32[4,8,8,192]{3,2,1,0:T(8,128)}, f32[4,8,8,192]{3,2,1,0:T(8,128)S(1)}, u32[]{:S(2)}) copy-start(f32[4,8,8,192]{3,2,1,0:T(8,128)S(1)} %collective-permute-done.6.refs_14_) | copy-start | bytes 589828
  64.6 2.9 %copy-start.12 = (f32[4,8,8,192]{3,2,1,0:T(8,128)}, f32[4,8,8,192]{3,2,1,0:T(8,128)S(1)}, u32[]{:S(2)}) copy-start(f32[4,8,8,192]{3,2,1,0:T(8,128)S(1)} %collective-permute-done.5.refs_13_) | copy-start | bytes 589828
  64.6 2.9 %copy-start.14 = (f32[4,8,8,192]{3,2,1,0:T(8,128)}, f32[4,8,8,192]{3,2,1,0:T(8,128)S(1)}, u32[]{:S(2)}) copy-start(f32[4,8,8,192]{3,2,1,0:T(8,128)S(1)} %collective-permute-done.4.refs_12_) | copy-start | bytes 589828
  64.6 24.7 %collective-permute-start.11 = (f32[4,8,8,192]{3,2,1,0:T(8,128)}, f32[4,8,8,192]{3,2,1,0:T(8,128)S(1)}, u32[]{:S(2)}, u32[]{:S(2)}) collective-permute-start(f32[4,8,8,192]{3,2,1,0:T(8,128)} %totals.3.refs_11_), channel_id=1, source_target_pairs={{0,3},{1,2},{2,1},{3,0},{4,7},{5,6},{6,5},{7,4},{8,11},{9,10},{10,... | collective-permute-start | bytes 589832 | tf_op jit(solution)/shard_map/ppermute | solution.py:289
  66.3 23.0 %collective-permute-start.10 = (f32[4,8,8,192]{3,2,1,0:T(8,128)}, f32[4,8,8,192]{3,2,1,0:T(8,128)S(1)}, u32[]{:S(2)}, u32[]{:S(2)}) collective-permute-start(f32[4,8,8,192]{3,2,1,0:T(8,128)} %totals.3.refs_11_), channel_id=1, source_target_pairs={{0,2},{1,3},{2,0},{3,1},{4,6},{5,7},{6,4},{7,5},{8,10},{9,11},{10,... | collective-permute-start | bytes 589832 | tf_op jit(solution)/shard_map/ppermute | solution.py:289
  66.4 22.9 %collective-permute-start.9 = (f32[4,8,8,192]{3,2,1,0:T(8,128)}, f32[4,8,8,192]{3,2,1,0:T(8,128)S(1)}, u32[]{:S(2)}, u32[]{:S(2)}) collective-permute-start(f32[4,8,8,192]{3,2,1,0:T(8,128)} %totals.3.refs_11_), channel_id=1, source_target_pairs={{0,1},{1,0},{2,3},{3,2},{4,5},{5,4},{6,7},{7,6},{8,9},{9,8},{10,11... | collective-permute-start | bytes 589832 | tf_op jit(solution)/shard_map/ppermute | solution.py:289
  89.3 0.7 copy-start.9
  89.3 0.8 copy-start.11
  89.3 0.8 copy-start.13
  90.2 42.6 %all-to-all-start = ((bf16[32,24,1536]{2,1,0:T(8,128)(2,1)}), bf16[32,24,1536]{2,1,0:T(8,128)(2,1)S(1)}, u32[]{:S(2)}, u32[]{:S(2)}) async-start(bf16[32,24,1536]{2,1,0:T(8,128)(2,1)} %bitcast.58), calls=%async_computation | async-start | bytes 4718592 | tf_op jit(solution)/shard_map/all_to_all | solution.py:337
  132.8 7.2 %collective-permute-start.12 = (bf16[2,8,192,128]{3,2,1,0:T(8,128)(2,1)}, bf16[2,8,192,128]{3,2,1,0:T(8,128)(2,1)}, u32[]{:S(2)}, u32[]{:S(2)}) collective-permute-start(bf16[2,8,192,128]{3,2,1,0:T(8,128)(2,1)} %get-tuple-element.63), channel_id=1, source_target_pairs={{0,1},{1,0},{2,3},{3,2},{4,5},{5,4},{6,7},{7,6},{8,9},{9,8},{10,11... | collective-permute-start | bytes 2359304 | tf_op jit(solution)/shard_map/ppermute | solution.py:289
  133.8 6.2 %copy-start.3 = (bf16[2,8,192,128]{3,2,1,0:T(8,128)(2,1)S(1)}, bf16[2,8,192,128]{3,2,1,0:T(8,128)(2,1)}, u32[]{:S(2)}) copy-start(bf16[2,8,192,128]{3,2,1,0:T(8,128)(2,1)} %get-tuple-element.62) | copy-start | bytes 2359300
  133.8 47.3 %all-to-all-start.1 = ((bf16[32,24,1536]{2,1,0:T(8,128)(2,1)}), bf16[32,24,1536]{2,1,0:T(8,128)(2,1)}, u32[]{:S(2)}, u32[]{:S(2)}) async-start(bf16[32,24,1536]{2,1,0:T(8,128)(2,1)} %bitcast.57), calls=%async_computation.1 | async-start | bytes 4718592 | tf_op jit(solution)/shard_map/all_to_all | solution.py:337
  141.5 34.8 %collective-permute-start.13 = (bf16[8,192,128]{2,1,0:T(8,128)(2,1)S(1)}, bf16[8,192,128]{2,1,0:T(8,128)(2,1)}, u32[]{:S(2)}, u32[]{:S(2)}) collective-permute-start(bf16[8,192,128]{2,1,0:T(8,128)(2,1)S(1)} %fusion.3), channel_id=1, source_target_pairs={{0,2},{1,3},{2,0},{3,1},{4,6},{5,7},{6,4},{7,5},{8,10},{9,11},{10,... | collective-permute-start | bytes 1179656 | tf_op jit(solution)/shard_map/ppermute | solution.py:289
  158.1 22.0 %copy-start.4 = (bf16[2,8,192,128]{3,2,1,0:T(8,128)(2,1)S(1)}, bf16[2,8,192,128]{3,2,1,0:T(8,128)(2,1)}, u32[]{:S(2)}) copy-start(bf16[2,8,192,128]{3,2,1,0:T(8,128)(2,1)} %get-tuple-element.73) | copy-start | bytes 2359300
  177.4 2.7 %collective-permute-start.14 = (bf16[2,8,192,128]{3,2,1,0:T(8,128)(2,1)}, bf16[2,8,192,128]{3,2,1,0:T(8,128)(2,1)S(1)}, u32[]{:S(2)}, u32[]{:S(2)}) collective-permute-start(bf16[2,8,192,128]{3,2,1,0:T(8,128)(2,1)} %get-tuple-element.74), channel_id=1, source_target_pairs={{0,1},{1,0},{2,3},{3,2},{4,5},{5,4},{6,7},{7,6},{8,9},{9,8},{10,11... | collective-permute-start | bytes 2359304 | tf_op jit(solution)/shard_map/ppermute | solution.py:289
  180.2 2.9 %copy-start.5 = (f32[24,1536]{1,0:T(8,128)S(1)}, f32[24,1536]{1,0:T(8,128)}, u32[]{:S(2)}) copy-start(f32[24,1536]{1,0:T(8,128)} %convert_reduce_fusion.1) | copy-start | bytes 442372
  180.3 10.4 %collective-permute-start.15 = (bf16[8,192,128]{2,1,0:T(8,128)(2,1)S(1)}, bf16[8,192,128]{2,1,0:T(8,128)(2,1)S(1)}, u32[]{:S(2)}, u32[]{:S(2)}) collective-permute-start(bf16[8,192,128]{2,1,0:T(8,128)(2,1)S(1)} %fusion.4), channel_id=1, source_target_pairs={{0,2},{1,3},{2,0},{3,1},{4,6},{5,7},{6,4},{7,5},{8,10},{9,11},{10,... | collective-permute-start | bytes 1179656 | tf_op jit(solution)/shard_map/ppermute | solution.py:289
